TPU v7x, 32 devices: a whole 2x2x4 slice. The times are simulated.
32 devices in a mesh: dp: 4 (over z), seq: 4 (over y, x), mp: 2 (over core).
Axes of the slice: x: 2, y: 2, z: 4, core: 2. Of those that a mesh axis runs over, the one named last changes fastest.
Arguments:
- residual: bfloat16 [6144, 3072], P(('dp', 'seq'), 'mp'), parts along dimension 0, may hold values from -10 to 10
- queries: bfloat16 [6144, 3072], P(('dp', 'seq', 'mp')), parts along dimension 0, may hold values from -6 to 6
- keys: bfloat16 [6144, 3072], P(('dp', 'seq', 'mp')), parts along dimension 0, may hold values from -6 to 6
- values: bfloat16 [6144, 3072], P(('dp', 'seq', 'mp')), parts along dimension 0, may hold values from -6 to 6
- video_ids: int32 [6144], P(('dp', 'seq', 'mp')), parts along dimension 0, may hold values from 0 to 3, never falling along the last dimension, each value on 1 to 768 neighbouring positions
- timestep: int32 [4], P('dp'), parts along dimension 0, may hold values from 0 to 49
- modulation: float32 [50, 3, 3072], P(None, None, 'mp'), may hold values from -4 to 4
- out_weight: bfloat16 [3072, 3072], P(None, 'mp'), may hold values from -0.109375 to 0.109375
Outputs:
- hidden_out: bfloat16 [6144, 3072], P(('dp', 'seq'), 'mp'), parts along dimension 0
- mlp_input: bfloat16 [6144, 3072], P(('dp', 'seq'), 'mp'), parts along dimension 0
There are 4 independent parts, one for each index of `dp`. A program takes and returns all parts, laid end to end along the dimension named above; an argument that names none is the same for every part. Nothing has to cross between parts.
Inputs may be any that keep to these rules, and one draw needn't show every extreme that they name: `video_ids`: video ids never fall along the tokens; each video holds 1 to 768 tokens and one holds exactly 768.
All inputs are finite; a program needn't handle non-finite values.
Results may differ from a plain program's by a relative error of at most 0.005.
Values may be sent and summed in bfloat16 or wider, within the bound.
A program may use at most 256 MiB of HBM per device.

v0:
```python
import jax
import jax.numpy as jnp
from jax import lax
from jax.sharding import PartitionSpec as P

HEAD_DIM = 128


def attend(carry, q_rows, q_ids, key_rows, value_rows, key_ids):
    top, total, summed = carry
    rows = q_rows.shape[0]
    count = key_rows.shape[0]
    heads = q_rows.shape[1] // HEAD_DIM
    factor = 1.0 / HEAD_DIM**0.5
    q_heads = q_rows.reshape(rows, heads, HEAD_DIM)
    k_heads = key_rows.reshape(count, heads, HEAD_DIM)
    v_heads = value_rows.reshape(count, heads, HEAD_DIM)
    same = (q_ids[:, None] == key_ids[None, :])[None]
    new_top, new_total, new_summed = ([], [], [])
    for first in range(0, heads, 3):
        score = (
            jnp.einsum(
                "thd,nhd->htn",
                q_heads[:, first : first + 3],
                k_heads[:, first : first + 3],
                preferred_element_type=jnp.float32,
            )
            * factor
        )
        score = jnp.where(same, score, -1e30)
        old_top = top[first : first + 3]
        peak = jnp.maximum(old_top, jnp.max(score, axis=2))
        weight = jnp.where(same, jnp.exp(score - peak[:, :, None]), 0.0)
        new_top.append(peak)
        new_total.append(jnp.sum(weight, axis=2))
        part_sum = jnp.einsum(
            "htn,nhd->htd",
            weight.astype(jnp.bfloat16),
            v_heads[:, first : first + 3],
            preferred_element_type=jnp.float32,
        )
        new_summed.append(part_sum)
    return (
        jnp.concatenate(new_top, 0),
        jnp.concatenate(new_total, 0),
        jnp.concatenate(new_summed, 0),
    )


def attend_maybe(carry, q_rows, q_ids, key_rows, value_rows, key_ids):
    return attend(carry, q_rows, q_ids, key_rows, value_rows, key_ids)


def start_state(q_rows):
    rows = q_rows.shape[0]
    heads = q_rows.shape[1] // HEAD_DIM
    return (
        jnp.full((heads, rows), -1e30, jnp.float32),
        jnp.zeros((heads, rows), jnp.float32),
        jnp.zeros((heads, rows, HEAD_DIM), jnp.float32),
    )


def finish(state, q_rows):
    top, total, summed = state
    rows = q_rows.shape[0]
    heads = q_rows.shape[1] // HEAD_DIM
    result = summed / total[:, :, None]
    return result.transpose(1, 0, 2).reshape(rows, heads * HEAD_DIM).astype(jnp.bfloat16)


def local(residual, queries, keys, values, video_ids, timestep, modulation, out_weight):
    steps_count = modulation.shape[0]
    picker = (jnp.arange(steps_count, dtype=jnp.int32) == timestep[0]).astype(jnp.float32)
    mod_rows = jnp.einsum("s,scd->cd", picker, modulation, precision=lax.Precision.HIGHEST)
    gate = mod_rows[0]
    shift = mod_rows[1]
    scale = mod_rows[2]
    width = queries.shape[1]
    state = attend_maybe(
        start_state(queries),
        queries,
        video_ids,
        lax.all_gather(keys, ("seq", "mp"), axis=0, tiled=True),
        lax.all_gather(values, ("seq", "mp"), axis=0, tiled=True),
        lax.all_gather(video_ids, ("seq", "mp"), axis=0, tiled=True),
    )
    attended = finish(state, queries)
    projected = jnp.dot(
        lax.all_gather(attended, "mp", axis=0, tiled=True),
        out_weight,
        preferred_element_type=jnp.float32,
    )
    stream = residual.astype(jnp.float32) + gate[None, :] * projected
    row_sum = jnp.sum(stream, axis=1, keepdims=True)
    row_sq = jnp.sum(stream * stream, axis=1, keepdims=True)
    row_sum, row_sq = lax.psum((row_sum, row_sq), "mp")
    mean = row_sum / width
    var = row_sq / width - mean * mean
    normed = (stream - mean) * lax.rsqrt(var + 1e-06) * (1.0 + scale[None, :]) + shift[None, :]
    return (stream.astype(jnp.bfloat16), normed.astype(jnp.bfloat16))


def solution(mesh):
    return jax.shard_map(
        local,
        mesh=mesh,
        in_specs=(
            P(("dp", "seq"), "mp"),
            P(("dp", "seq", "mp"), None),
            P(("dp", "seq", "mp"), None),
            P(("dp", "seq", "mp"), None),
            P(("dp", "seq", "mp")),
            P("dp"),
            P(None, None, "mp"),
            P(None, "mp"),
        ),
        out_specs=(P(("dp", "seq"), "mp"), P(("dp", "seq"), "mp")),
        check_vma=False,
    )
```

profile of v0, /device:TPU:0, one launch (start us, length us, event | category | flops | bytes accessed | tf_op | source)
XLA Modules:
  0.0 205.6 jit_solution(1597267509583217930)
XLA Ops:
  7.2 0.0 copy-start
  7.2 0.0 copy-start.12
  7.2 0.0 copy-start.11
  7.2 0.0 all-gather.4.cloned.1.call-start
  7.2 0.7 all-gather.4.cloned.1.call-update
  7.9 0.0 all-gather.6.cloned.1.call-start
  8.0 0.7 all-gather.6.cloned.1.call-update
  8.7 0.0 all-gather.8.cloned.1.call-start
  8.7 1.5 copy.90
  10.2 0.0 copy-done.12
  10.2 0.6 dynamic-slice
  11.5 0.0 copy-done.11
  11.5 0.3 dynamic-update-slice
  11.8 9.6 %all-reduce = s32[1536]{0:T(1024)S(1)} all-reduce(s32[1536]{0:T(1024)S(1)} %dynamic-update-slice), channel_id=1, replica_groups=mesh['dp'=4,'seq'=4,'mp'=2] {'seq','mp'}, use_global_device_ids=true, to_apply=%add | all-reduce | flops 1536 | bytes 12288
  21.3 1.4 fusion.121
  22.8 0.2 broadcast_compare_fusion
  23.0 0.0 copy-start.10
  23.0 48.5 %all-gather.4.cloned.1.call-done = bf16[1536,3072]{1,0:T(8,128)(2,1)} async-done(((bf16[192,3072]{1,0:T(8,128)(2,1)}), bf16[1536,3072]{1,0:T(8,128)(2,1)}) %all-gather.4.cloned.1.call-update) | async-done | bytes 9437200 | tf_op jit(solution)/shard_map/all_gather | solution.py:84
  71.5 12.8 %copy.38 = bf16[1536,3072]{0,1:T(8,128)(2,1)} copy(bf16[1536,3072]{1,0:T(8,128)(2,1)} %all-gather.4.cloned.1.call-done) | data formatting | bytes 18874368 | tf_op jit(solution)/shard_map/all_gather | solution.py:84
  84.2 0.0 copy-start.9
  84.3 0.0 copy-done.10
  84.3 4.1 %fusion.128 = (f32[3,192]{1,0:T(4,128)S(1)}, f32[3,192,1536]{2,1,0:T(8,128)}) fusion(bf16[1536,24,128]{0,2,1:T(8,128)(2,1)} %bitcast.30, bf16[192,3,128]{2,1,0:T(4,128)(2,1)S(1)} %copy-done.10, pred[192,1536]{1,0:T(8,128)(4,1)S(1)} %broadcast_compare_fusion), kind=kOutput, calls=%fused_computation.140 | convolution fusion | flops 229146048 | bytes 5163264 | tf_op jit(solution)/shard_map/thd,nhd->htn/dot_general | solution.py:22
  88.4 0.0 copy-done.9
  88.4 4.2 %fusion.129 = (f32[3,192]{1,0:T(4,128)S(1)}, f32[3,192,1536]{2,1,0:T(8,128)}) fusion(bf16[1536,24,128]{0,2,1:T(8,128)(2,1)} %bitcast.31, bf16[192,3,128]{2,1,0:T(4,128)(2,1)S(1)} %copy-done.9, pred[192,1536]{1,0:T(8,128)(4,1)S(1)} %broadcast_compare_fusion), kind=kOutput, calls=%fused_computation.141 | convolution fusion | flops 229146048 | bytes 5163264 | tf_op jit(solution)/shard_map/thd,nhd->htn/dot_general | solution.py:22
  92.6 0.0 copy-done.2
  92.6 2.6 %fusion.126 = (f32[3,192]{1,0:T(4,128)S(1)}, f32[3,192,1536]{2,1,0:T(8,128)}) fusion(bf16[1536,24,128]{0,2,1:T(8,128)(2,1)S(1)} %bitcast.32, bf16[192,3,128]{2,1,0:T(4,128)(2,1)S(1)} %get-tuple-element.24, pred[192,1536]{1,0:T(8,128)(4,1)S(1)} %broadcast_compare_fusion), kind=kOutput, calls=%fused_computation.138 | convolution fusion | flops 229146048 | bytes 5212416 | tf_op jit(solution)/shard_map/thd,nhd->htn/dot_general | solution.py:22
  95.2 2.6 %fusion.127 = (f32[3,192]{1,0:T(4,128)S(1)}, f32[3,192,1536]{2,1,0:T(8,128)}) fusion(bf16[1536,24,128]{0,2,1:T(8,128)(2,1)S(1)} %bitcast.33, bf16[192,3,128]{2,1,0:T(4,128)(2,1)S(1)} %get-tuple-element.23, pred[192,1536]{1,0:T(8,128)(4,1)S(1)} %broadcast_compare_fusion), kind=kOutput, calls=%fused_computation.139 | convolution fusion | flops 229146048 | bytes 5212416 | tf_op jit(solution)/shard_map/thd,nhd->htn/dot_general | solution.py:22
  97.9 2.7 %fusion.124 = (f32[3,192]{1,0:T(4,128)S(1)}, f32[3,192,1536]{2,1,0:T(8,128)}) fusion(bf16[1536,24,128]{0,2,1:T(8,128)(2,1)S(1)} %bitcast.34, bf16[192,3,128]{2,1,0:T(4,128)(2,1)S(1)} %get-tuple-element.26, pred[192,1536]{1,0:T(8,128)(4,1)S(1)} %broadcast_compare_fusion), kind=kOutput, calls=%fused_computation.136 | convolution fusion | flops 229146048 | bytes 5212416 | tf_op jit(solution)/shard_map/thd,nhd->htn/dot_general | solution.py:22
  100.6 2.7 %fusion.125 = (f32[3,192]{1,0:T(4,128)S(1)}, f32[3,192,1536]{2,1,0:T(8,128)}) fusion(bf16[1536,24,128]{0,2,1:T(8,128)(2,1)S(1)} %bitcast.35, bf16[192,3,128]{2,1,0:T(4,128)(2,1)S(1)} %get-tuple-element.25, pred[192,1536]{1,0:T(8,128)(4,1)S(1)} %broadcast_compare_fusion), kind=kOutput, calls=%fused_computation.137 | convolution fusion | flops 229146048 | bytes 5212416 | tf_op jit(solution)/shard_map/thd,nhd->htn/dot_general | solution.py:22
  103.3 2.6 %fusion.122 = (f32[3,192]{1,0:T(4,128)S(1)}, f32[3,192,1536]{2,1,0:T(8,128)}) fusion(bf16[1536,24,128]{0,2,1:T(8,128)(2,1)S(1)} %bitcast.36, bf16[192,3,128]{2,1,0:T(4,128)(2,1)S(1)} %get-tuple-element.28, pred[192,1536]{1,0:T(8,128)(4,1)S(1)} %broadcast_compare_fusion), kind=kOutput, calls=%fused_computation.134 | convolution fusion | flops 229146048 | bytes 5212416 | tf_op jit(solution)/shard_map/thd,nhd->htn/dot_general | solution.py:22
  105.9 2.6 %fusion.123 = (f32[3,192]{1,0:T(4,128)S(1)}, f32[3,192,1536]{2,1,0:T(8,128)}) fusion(bf16[1536,24,128]{0,2,1:T(8,128)(2,1)S(1)} %bitcast.37, bf16[192,3,128]{2,1,0:T(4,128)(2,1)S(1)} %get-tuple-element.27, pred[192,1536]{1,0:T(8,128)(4,1)S(1)} %broadcast_compare_fusion), kind=kOutput, calls=%fused_computation.135 | convolution fusion | flops 229146048 | bytes 5212416 | tf_op jit(solution)/shard_map/thd,nhd->htn/dot_general | solution.py:22
  108.5 23.7 %all-gather.6.cloned.1.call-done = bf16[1536,3072]{1,0:T(8,128)(2,1)} async-done(((bf16[192,3072]{1,0:T(8,128)(2,1)}), bf16[1536,3072]{1,0:T(8,128)(2,1)}) %all-gather.6.cloned.1.call-update) | async-done | bytes 9437200 | tf_op jit(solution)/shard_map/all_gather | solution.py:85
  132.2 12.7 %copy.40 = bf16[1536,3072]{0,1:T(8,128)(2,1)} copy(bf16[1536,3072]{1,0:T(8,128)(2,1)} %all-gather.6.cloned.1.call-done) | data formatting | bytes 18874368 | tf_op jit(solution)/shard_map/all_gather | solution.py:85
  144.9 0.0 copy-start.1
  144.9 3.9 %fusion.57 = f32[24,192,128]{2,1,0:T(8,128)} fusion(f32[3,192,1536]{2,1,0:T(8,128)} %get-tuple-element.30, f32[3,192]{1,0:T(4,128)S(1)} %get-tuple-element.53, pred[192,1536]{1,0:T(8,128)(4,1)S(1)} %broadcast_compare_fusion, bf16[1536,24,128]{0,2,1:T(8,128)(2,1)} %bitcast.22), kind=kOutput, calls=%fused_computation.69 | convolution fusion | flops 229146624 | bytes 5310720 | tf_op jit(solution)/shard_map/htn,nhd->htd/dot_general | solution.py:36
  148.9 0.0 copy-start.7
  148.9 4.1 %fusion.60 = f32[24,192,128]{2,1,0:T(8,128)} fusion(f32[24,192,128]{2,1,0:T(8,128)} %fusion.57, f32[3,192,1536]{2,1,0:T(8,128)} %get-tuple-element.32, f32[3,192]{1,0:T(4,128)S(1)} %get-tuple-element.52, pred[192,1536]{1,0:T(8,128)(4,1)S(1)} %broadcast_compare_fusion, bf16[1536,24,128]{0,2,1:T(8,128)(2,1)} %bitcast.23), kind=kOutput, calls=%fused_computation.70 | convolution fusion | flops 229146624 | bytes 5310720 | tf_op jit(solution)/shard_map/htn,nhd->htd/dot_general | solution.py:36
  152.9 0.0 copy-start.8
  152.9 0.0 copy-done.1
  152.9 0.0 copy-done.7
  153.0 1.5 fusion.63
  154.4 0.0 copy-start.5
  154.4 0.6 copy-done.8
  155.1 1.5 fusion.66
  156.5 0.0 copy-start.6
  156.5 0.1 copy-done.5
  156.6 1.5 fusion.69
  158.1 0.6 copy-done.6
  158.7 1.5 fusion.72
  160.1 0.1 copy-done.4
  160.2 1.5 fusion.75
  161.7 0.5 copy-done.3
  162.3 7.8 %fusion.15 = (f32[3,192]{1,0:T(4,128)S(1)}, f32[3,192]{1,0:T(4,128)S(1)}, f32[3,192]{1,0:T(4,128)S(1)}, f32[3,192]{1,0:T(4,128)S(1)}, f32[3,192]{1,0:T(4,128)S(1...) fusion(f32[3,192,1536]{2,1,0:T(8,128)S(1)} %copy-done.3, f32[3,192]{1,0:T(4,128)S(1)} %get-tuple-element.46, ...), kind=kLoop, calls=%fused_computation.32 | loop fusion | flops 21229056 | bytes 28643328 | tf_op jit(solution)/shard_map/reduce_sum | solution.py:35
  170.1 1.5 fusion.78
  171.6 0.2 concatenate.7
  171.8 2.9 %copy_bitcast_fusion = bf16[192,3072]{1,0:T(8,128)(2,1)} fusion(f32[24,192,128]{2,1,0:T(8,128)} %fusion.78, f32[24,192]{1,0:T(8,128)S(1)} %concatenate.7), kind=kLoop, calls=%fused_computation.77 | loop fusion | flops 1179648 | bytes 3557376 | tf_op jit(solution)/shard_map/convert_element_type | solution.py:69
  174.8 0.0 all-gather.8.cloned.1.call-update
  175.4 0.0 copy-done
  175.5 0.4 fusion.107
  175.9 0.1 fusion.106
  176.0 9.9 %all-gather.8.cloned.1.call-done = bf16[384,3072]{1,0:T(8,128)(2,1)} async-done(((bf16[192,3072]{1,0:T(8,128)(2,1)}), bf16[384,3072]{1,0:T(8,128)(2,1)}) %all-gather.8.cloned.1.call-update) | async-done | bytes 2359312 | tf_op jit(solution)/shard_map/all_gather | solution.py:90
  185.9 8.6 %fusion.120 = (f32[384]{0:T(512)S(1)}, f32[384]{0:T(512)S(1)}, f32[384,1536]{1,0:T(8,128)S(1)}) fusion(bf16[384,3072]{1,0:T(8,128)(2,1)} %all-gather.8.cloned.1.call-done, bf16[3072,1536]{1,0:T(8,128)(2,1)} %param.15, f32[1536]{0:T(1024)S(1)} %get-tuple-element.14, bf16[384,1536]{1,0:T(8,128)(2,1)} %param.8), kind=kOutput, calls=%fused_computation.132 | convolution fusion | flops 3627416576 | bytes 15344640 | tf_op jit(solution)/shard_map/dot_general | solution.py:89
  194.6 2.5 %all-reduce.1 = (f32[384,1]{0,1:T(1,128)S(1)}, f32[384,1]{0,1:T(1,128)S(1)}) all-reduce(f32[384,1]{0,1:T(1,128)S(1)} %broadcast_in_dim.95, f32[384,1]{0,1:T(1,128)S(1)} %broadcast_in_dim.96), channel_id=1, replica_groups=mesh['dp'=4,'seq'=4,'mp'=2] {'mp'}, use_global_device_ids=true, to_apply=%region_17.18 | all-reduce | flops 768 | bytes 6144 | tf_op jit(solution)/shard_map/psum | solution.py:97
  197.1 2.0 add_convert_fusion
  (12 shorter events, 0.1 us)
Async XLA Ops:
  7.2 168.3 %copy-start = (f32[50,3,1536]{2,0,1:T(8,128)S(1)}, f32[50,3,1536]{2,0,1:T(8,128)}, u32[]{:S(2)}) copy-start(f32[50,3,1536]{2,0,1:T(8,128)} %param.14) | copy-start | bytes 2764804
  7.2 3.1 %copy-start.12 = (u32[32]{0:T(128)S(1)}, u32[32]{0:T(128)}, u32[]{:S(2)}) copy-start(u32[32]{0:T(128)} %constant.20) | copy-start | bytes 388
  7.2 4.3 %copy-start.11 = (s32[192]{0:T(256)S(1)}, s32[192]{0:T(256)}, u32[]{:S(2)}) copy-start(s32[192]{0:T(256)} %param.12) | copy-start | bytes 2308
  7.2 64.3 %all-gather.4.cloned.1.call-start = ((), (), s32[]{:S(2)}) async-start(), calls=%async_computation | async-start | bytes 10616832 | tf_op jit(solution)/shard_map/all_gather | solution.py:84
  7.9 124.3 %all-gather.6.cloned.1.call-start = ((), (), s32[]{:S(2)}) async-start(), calls=%async_computation.1 | async-start | bytes 10616832 | tf_op jit(solution)/shard_map/all_gather | solution.py:85
  8.7 177.2 %all-gather.8.cloned.1.call-start = ((), (), s32[]{:S(2)}) async-start(), calls=%async_computation.2 | async-start | bytes 3538944 | tf_op jit(solution)/shard_map/all_gather | solution.py:90
  23.0 61.2 %copy-start.10 = (bf16[192,3,128]{2,1,0:T(4,128)(2,1)S(1)}, bf16[192,3,128]{2,1,0:T(4,128)(2,1)}, u32[]{:S(2)}) copy-start(bf16[192,3,128]{2,1,0:T(4,128)(2,1)} %get-tuple-element.22) | copy-start | bytes 442372
  84.2 4.1 %copy-start.9 = (bf16[192,3,128]{2,1,0:T(4,128)(2,1)S(1)}, bf16[192,3,128]{2,1,0:T(4,128)(2,1)}, u32[]{:S(2)}) copy-start(bf16[192,3,128]{2,1,0:T(4,128)(2,1)} %get-tuple-element.21) | copy-start | bytes 442372
  84.3 8.3 %copy-start.2 = (bf16[1536,3072]{0,1:T(8,128)(2,1)S(1)}, bf16[1536,3072]{0,1:T(8,128)(2,1)}, u32[]{:S(2)}) copy-start(bf16[1536,3072]{0,1:T(8,128)(2,1)} %copy.38) | copy-start | bytes 28311556
  144.9 8.0 %copy-start.1 = (bf16[1536,3072]{0,1:T(8,128)(2,1)S(1)}, bf16[1536,3072]{0,1:T(8,128)(2,1)}, u32[]{:S(2)}) copy-start(bf16[1536,3072]{0,1:T(8,128)(2,1)} %copy.40) | copy-start | bytes 28311556
  148.9 4.1 %copy-start.7 = (f32[3,192,1536]{2,1,0:T(8,128)S(1)}, f32[3,192,1536]{2,1,0:T(8,128)}, u32[]{:S(2)}) copy-start(f32[3,192,1536]{2,1,0:T(8,128)} %get-tuple-element.34) | copy-start | bytes 10616836
  152.9 2.1 %copy-start.8 = (f32[3,192,1536]{2,1,0:T(8,128)S(1)}, f32[3,192,1536]{2,1,0:T(8,128)}, u32[]{:S(2)}) copy-start(f32[3,192,1536]{2,1,0:T(8,128)} %get-tuple-element.36) | copy-start | bytes 10616836
  154.4 2.2 %copy-start.5 = (f32[3,192,1536]{2,1,0:T(8,128)S(1)}, f32[3,192,1536]{2,1,0:T(8,128)}, u32[]{:S(2)}) copy-start(f32[3,192,1536]{2,1,0:T(8,128)} %get-tuple-element.38) | copy-start | bytes 10616836
  156.5 2.1 %copy-start.6 = (f32[3,192,1536]{2,1,0:T(8,128)S(1)}, f32[3,192,1536]{2,1,0:T(8,128)}, u32[]{:S(2)}) copy-start(f32[3,192,1536]{2,1,0:T(8,128)} %get-tuple-element.40) | copy-start | bytes 10616836
  158.1 2.1 %copy-start.4 = (f32[3,192,1536]{2,1,0:T(8,128)S(1)}, f32[3,192,1536]{2,1,0:T(8,128)}, u32[]{:S(2)}) copy-start(f32[3,192,1536]{2,1,0:T(8,128)} %get-tuple-element.42) | copy-start | bytes 10616836
  160.1 2.1 %copy-start.3 = (f32[3,192,1536]{2,1,0:T(8,128)S(1)}, f32[3,192,1536]{2,1,0:T(8,128)}, u32[]{:S(2)}) copy-start(f32[3,192,1536]{2,1,0:T(8,128)} %get-tuple-element.44) | copy-start | bytes 10616836
Sparse Core Ops, SparseCore 0:
  9.9 61.5 all-gather.3
  73.4 58.8 all-gather.5
  174.9 10.9 all-gather.7
where the time goes:
time: 207 us; the launch traced here: 206 us
  waiting for transfers between devices  83.5 us (40%)
  matrix products  50.3 us (24%)
  local copies, waits for them, and re-layouts  31.4 us (15%)
  between operations  15.2 us (7%)
  other arithmetic  13.1 us (6%)
  blocking collectives  12 us (6%)
    all_gather x1, waiting for transfers between devices, local(): lax.all_gather(keys, ('seq', 'mp'), axis=0, tiled=True)  48.5 us
    dot_general x8, matrix products, attend(): jnp.einsum('thd,nhd->htn', q_heads[:, first:first + 3], k_heads[:, first:...  24.2 us
    all_gather x1, waiting for transfers between devices, local(): lax.all_gather(values, ('seq', 'mp'), axis=0, tiled=True)  23.7 us
    dot_general x8, matrix products, attend(): jnp.einsum('htn,nhd->htd', weight.astype(jnp.bfloat16), v_heads[:, first:...  17 us
    all_gather x1, local copies, waits for them, and re-layouts, local(): lax.all_gather(keys, ('seq', 'mp'), axis=0, tiled=True)  12.8 us
    all_gather x1, local copies, waits for them, and re-layouts, local(): lax.all_gather(values, ('seq', 'mp'), axis=0, tiled=True)  12.7 us
    all_gather x1, waiting for transfers between devices, local(): lax.all_gather(attended, 'mp', axis=0, tiled=True)  9.94 us
    unnamed x1, blocking collectives  9.55 us
  transfers between devices with their start and end apart: 3, of which 3 were waited for; matrix products, arithmetic and copies ran while one was open for 20% of the time, Pallas kernels for 0%

commit v1 on v0

--- a/solution.py
+++ b/solution.py
@@ -1,9 +1,317 @@
+import functools
+import math
+
 import jax
 import jax.numpy as jnp
 from jax import lax
+from jax.experimental import pallas as pl
+from jax.experimental.pallas import tpu as pltpu
 from jax.sharding import PartitionSpec as P
 
 HEAD_DIM = 128
+VIDEOS = 4
+MESH = pl.DeviceIdType.MESH
+
+
+def rows_at(index, count):
+    return pl.ds(pl.multiple_of(index * count, count), count)
+
+
+def whole(ref, sem):
+    return pltpu.make_async_copy(ref, ref, sem)
+
+
+def fused_kernel(
+    n, mp_n, width,
+    q_ref, k_ref, v_ref, ids_ref, mod_ref, res_ref, w_ref,
+    hid_ref, mlp_ref,
+    qkv, obuf, att, wbuf, res, acc, hid, mlp, counts, stat_mine, stat_other,
+    qkv_send, qkv_recv, o_send, o_recv, fwd_send, fwd_recv,
+    cnt_send, cnt_recv, stat_send, stat_recv, w_sem, res_sem, out_sem,
+):
+    seq_i = lax.axis_index("seq")
+    mp_i = lax.axis_index("mp")
+    me = seq_i * mp_n + mp_i
+    rows = q_ref.shape[0]
+    groups = qkv.shape[0]
+    tokens = qkv.shape[2]
+    columns = w_ref.shape[1]
+    sibling = {"mp": 1 - mp_i}
+
+    def device(p):
+        return {"seq": lax.div(p, mp_n), "mp": lax.rem(p, mp_n)}
+
+    def each_peer(body):
+        def step(d, carry):
+            body(lax.rem(me + d, n))
+            return carry
+
+        lax.fori_loop(1, n, step, 0)
+
+    def load_weight(g, p):
+        return pltpu.make_async_copy(
+            w_ref.at[rows_at(p * groups + g, HEAD_DIM)],
+            wbuf.at[g, rows_at(p, HEAD_DIM)],
+            w_sem.at[g],
+        )
+
+    load_res = pltpu.make_async_copy(res_ref, res, res_sem)
+
+    ids = ids_ref[...]
+    below = [
+        jnp.sum((ids <= k).astype(jnp.float32), axis=1, keepdims=True)
+        for k in range(VIDEOS - 1)
+    ]
+    line = lax.broadcasted_iota(jnp.int32, (8, 128), 0)
+    mine = jnp.where(line == 0, below[0], jnp.where(line == 1, below[1], below[2]))
+    counts[rows_at(me, 8), :] = mine
+
+    barrier = pltpu.get_barrier_semaphore()
+    each_peer(
+        lambda p: pl.semaphore_signal(
+            barrier, inc=1, device_id=device(p), device_id_type=MESH
+        )
+    )
+    pl.semaphore_wait(barrier, n - 1)
+
+    def send_count(p):
+        pltpu.make_async_remote_copy(
+            src_ref=counts.at[rows_at(me, 8)],
+            dst_ref=counts.at[rows_at(me, 8)],
+            send_sem=cnt_send,
+            recv_sem=cnt_recv,
+            device_id=device(p),
+            device_id_type=MESH,
+        ).start()
+
+    each_peer(send_count)
+
+    def send_group(g):
+        for t, ref in enumerate((k_ref, q_ref, v_ref)):
+
+            def send(p, ref=ref, t=t):
+                pltpu.make_async_remote_copy(
+                    src_ref=ref.at[:, rows_at(p * groups + g, HEAD_DIM)],
+                    dst_ref=qkv.at[g, t, rows_at(me, rows)],
+                    send_sem=qkv_send.at[g],
+                    recv_sem=qkv_recv.at[g],
+                    device_id=device(p),
+                    device_id_type=MESH,
+                ).start()
+
+            each_peer(send)
+            pltpu.make_async_copy(
+                ref.at[:, rows_at(me * groups + g, HEAD_DIM)],
+                qkv.at[g, t, rows_at(me, rows)],
+                qkv_recv.at[g],
+            ).start()
+
+    def attention(g, totals):
+        lane = lax.broadcasted_iota(jnp.int32, (1, tokens), 1).astype(jnp.float32)
+        key_ids = sum((lane >= c).astype(jnp.float32) for c in totals)
+        tile = 2 * HEAD_DIM
+        factor = math.log2(math.e) / HEAD_DIM**0.5
+
+        def step(i, carry):
+            at = rows_at(i, tile)
+            place = (lax.broadcasted_iota(jnp.int32, (tile, 1), 0) + i * tile).astype(
+                jnp.float32
+            )
+            own_ids = sum((place >= c).astype(jnp.float32) for c in totals)
+            score = lax.dot_general(
+                qkv[g, 1, at, :],
+                qkv[g, 0],
+                (((1,), (1,)), ((), ())),
+                preferred_element_type=jnp.float32,
+            )
+            score = jnp.where(own_ids == key_ids, score, -1e30)
+            top = jnp.max(score, axis=1, keepdims=True)
+            weight = jnp.exp2((score - top) * factor)
+            total = jnp.sum(weight, axis=1, keepdims=True)
+            summed = jnp.dot(
+                weight.astype(jnp.bfloat16),
+                qkv[g, 2],
+                preferred_element_type=jnp.float32,
+            )
+            obuf[g, at, :] = (summed / total).astype(jnp.bfloat16)
+            return carry
+
+        lax.fori_loop(0, tokens // tile, step, 0)
+
+    def send_back(g):
+        def send(p):
+            pltpu.make_async_remote_copy(
+                src_ref=obuf.at[g, rows_at(p, rows)],
+                dst_ref=att.at[
+                    g, rows_at(lax.rem(p, mp_n), rows), rows_at(me, HEAD_DIM)
+                ],
+                send_sem=o_send.at[g],
+                recv_sem=o_recv.at[g],
+                device_id=device(p),
+                device_id_type=MESH,
+            ).start()
+
+        each_peer(send)
+        pltpu.make_async_copy(
+            obuf.at[g, rows_at(me, rows)],
+            att.at[g, rows_at(mp_i, rows), rows_at(me, HEAD_DIM)],
+            o_recv.at[g],
+        ).start()
+
+    def forward(g):
+        half = att.at[g, rows_at(mp_i, rows)]
+        return pltpu.make_async_remote_copy(
+            src_ref=half,
+            dst_ref=half,
+            send_sem=fwd_send.at[g],
+            recv_sem=fwd_recv.at[g],
+            device_id=sibling,
+            device_id_type=MESH,
+        )
+
+    def pass_on(g):
+        whole(att.at[g, rows_at(mp_i, rows)], o_recv.at[g]).wait()
+        forward(g).start()
+
+    def project(g):
+        whole(wbuf.at[g], w_sem.at[g]).wait()
+        whole(att.at[g, rows_at(1 - mp_i, rows)], fwd_recv.at[g]).wait()
+        tile = 2 * HEAD_DIM
+
+        def step(i, carry):
+            at = rows_at(i, tile)
+            part = jnp.dot(
+                att[g], wbuf[g, :, at], preferred_element_type=jnp.float32
+            )
+            acc[:, at] = part if g == 0 else acc[:, at] + part
+            return carry
+
+        lax.fori_loop(0, columns // tile, step, 0)
+
+    send_group(0)
+    if groups > 1:
+        send_group(1)
+    load_res.start()
+    for g in range(groups):
+
+        def start_load(p, carry, g=g):
+            load_weight(g, p).start()
+            return carry
+
+        lax.fori_loop(0, n, start_load, 0)
+    whole(counts.at[pl.ds(0, 8 * (n - 1))], cnt_recv).wait()
+    sums = counts[pl.ds(0, 8), :]
+    for r in range(1, n):
+        sums = sums + counts[pl.ds(8 * r, 8), :]
+    totals = [sums[k : k + 1, 0:1] for k in range(VIDEOS - 1)]
+
+    for g in range(groups):
+        whole(qkv.at[g], qkv_recv.at[g]).wait()
+        if g + 2 < groups:
+            send_group(g + 2)
+        attention(g, totals)
+        send_back(g)
+        if g >= 1:
+            pass_on(g - 1)
+        if g >= 2:
+            project(g - 2)
+    if groups >= 2:
+        project(groups - 2)
+    pass_on(groups - 1)
+    project(groups - 1)
+
+    load_res.wait()
+    gate = mod_ref[0:1, :]
+    shift = mod_ref[1:2, :]
+    scale = 1.0 + mod_ref[2:3, :]
+    high = acc.shape[0]
+    tile = 64
+    side = lax.broadcasted_iota(jnp.int32, (tile, 128), 1) < 64
+
+    def gated(i, carry):
+        at = rows_at(i, tile)
+        stream = res[at, :].astype(jnp.float32) + gate * acc[at, :]
+        acc[at, :] = stream
+        hid[at, :] = stream.astype(jnp.bfloat16)
+        row_sum = jnp.sum(stream, axis=1, keepdims=True)
+        row_sq = jnp.sum(stream * stream, axis=1, keepdims=True)
+        stat_mine[at, :] = jnp.where(side, row_sum, row_sq)
+        return carry
+
+    lax.fori_loop(0, high // tile, gated, 0)
+    stats = pltpu.make_async_remote_copy(
+        src_ref=stat_mine,
+        dst_ref=stat_other,
+        send_sem=stat_send,
+        recv_sem=stat_recv,
+        device_id=sibling,
+        device_id_type=MESH,
+    )
+    stats.start()
+    store_hid = pltpu.make_async_copy(hid, hid_ref, out_sem.at[0])
+    store_hid.start()
+    stats.wait_recv()
+
+    def normed(i, carry):
+        at = rows_at(i, tile)
+        both = stat_mine[at, :] + stat_other[at, :]
+        mean = both[:, 0:1] / width
+        var = both[:, 64:65] / width - mean * mean
+        stream = acc[at, :]
+        result = (stream - mean) * lax.rsqrt(var + 1e-06) * scale + shift
+        mlp[at, :] = result.astype(jnp.bfloat16)
+        return carry
+
+    lax.fori_loop(0, high // tile, normed, 0)
+    store_mlp = pltpu.make_async_copy(mlp, mlp_ref, out_sem.at[1])
+    store_mlp.start()
+
+    stats.wait_send()
+    whole(counts.at[pl.ds(0, 8 * (n - 1))], cnt_send).wait()
+    for g in range(groups):
+        whole(qkv.at[g, :, pl.ds(0, rows * (n - 1))], qkv_send.at[g]).wait()
+        whole(obuf.at[g, pl.ds(0, rows * (n - 1))], o_send.at[g]).wait()
+        forward(g).wait_send()
+    store_hid.wait()
+    store_mlp.wait()
+
+
+def fused(n, mp_n, residual, queries, keys, values, video_ids, timestep, modulation, out_weight):
+    mod_rows = lax.dynamic_index_in_dim(modulation, timestep[0], 0, keepdims=False)
+    rows, width = queries.shape
+    high, columns = residual.shape
+    tokens = rows * n
+    groups = width // HEAD_DIM // n
+    bf16 = jnp.bfloat16
+    dma = pltpu.SemaphoreType.DMA
+    anywhere = pl.BlockSpec(memory_space=pl.ANY)
+    vmem = pl.BlockSpec(memory_space=pltpu.VMEM)
+    out = jax.ShapeDtypeStruct(residual.shape, bf16)
+    return pl.pallas_call(
+        functools.partial(fused_kernel, n, mp_n, width),
+        out_shape=(out, out),
+        in_specs=[anywhere, anywhere, anywhere, vmem, vmem, anywhere, anywhere],
+        out_specs=(anywhere, anywhere),
+        scratch_shapes=[
+            pltpu.VMEM((groups, 3, tokens, HEAD_DIM), bf16),
+            pltpu.VMEM((groups, tokens, HEAD_DIM), bf16),
+            pltpu.VMEM((groups, high, n * HEAD_DIM), bf16),
+            pltpu.VMEM((groups, n * HEAD_DIM, columns), bf16),
+            pltpu.VMEM((high, columns), bf16),
+            pltpu.VMEM((high, columns), jnp.float32),
+            pltpu.VMEM((high, columns), bf16),
+            pltpu.VMEM((high, columns), bf16),
+            pltpu.VMEM((8 * n, 128), jnp.float32),
+            pltpu.VMEM((high, 128), jnp.float32),
+            pltpu.VMEM((high, 128), jnp.float32),
+            dma((groups,)), dma((groups,)), dma((groups,)), dma((groups,)),
+            dma((groups,)), dma((groups,)),
+            dma, dma, dma, dma, dma((groups,)), dma, dma((2,)),
+        ],
+        compiler_params=pltpu.CompilerParams(
+            collective_id=0, has_side_effects=True, vmem_limit_bytes=52 * 2**20
+        ),
+    )(queries, keys, values, video_ids.reshape(1, rows), mod_rows, residual, out_weight)
 
 
 def attend(carry, q_rows, q_ids, key_rows, value_rows, key_ids):
@@ -101,9 +409,23 @@
     return (stream.astype(jnp.bfloat16), normed.astype(jnp.bfloat16))
 
 
+def choose(mesh):
+    seq_n, mp_n = mesh.shape["seq"], mesh.shape["mp"]
+    n = seq_n * mp_n
+
+    def run(*arrays):
+        queries = arrays[1]
+        rows, width = queries.shape
+        if mp_n == 2 and width // HEAD_DIM % n == 0 and rows % 64 == 0 and rows * n % 256 == 0:
+            return fused(n, mp_n, *arrays)
+        return local(*arrays)
+
+    return run
+
+
 def solution(mesh):
     return jax.shard_map(
-        local,
+        choose(mesh),
         mesh=mesh,
         in_specs=(
             P(("dp", "seq"), "mp"),

time: 207 us -> 74.4 us (0.36)
  waiting for transfers between devices: 83.5 us -> 0 us
  Pallas kernels: 0 us -> 68.6 us
  matrix products: 50.3 us -> 0 us
  local copies, waits for them, and re-layouts: 31.4 us -> 3.9 us
  between operations: 15.2 us -> 1.41 us
  other arithmetic: 13.1 us -> 0 us
  blocking collectives: 12 us -> 0 us
    all_gather x3 -> x0, waiting for transfers between devices: 82.1 us -> none  [the longest x1 48.5 us: local(): lax.all_gather(keys, ('seq', 'mp'), axis=0, tiled=True)]
    pallas_call x0 -> x1, Pallas kernels: none -> 68.6 us  [fused(): pl.pallas_call(functools.partial(fused_kernel, n, mp_n, width), out_shape...]
    dot_general x18 -> x0, matrix products: 50.3 us -> none  [the longest x8 24.2 us: attend(): jnp.einsum('thd,nhd->htn', q_heads[:, first:first + 3], k_heads[:, first:...]
    all_gather x2 -> x0, local copies, waits for them, and re-layouts: 25.5 us -> none  [the longest x1 12.8 us: local(): lax.all_gather(keys, ('seq', 'mp'), axis=0, tiled=True)]
    unnamed x1 -> x0, blocking collectives: 9.55 us -> none
    reduce_sum x1 -> x0, other arithmetic: 7.82 us -> none  [attend(): new_total.append(jnp.sum(weight, axis=2))]
    convert_element_type x2 -> x0, other arithmetic: 4.94 us -> none  [the longest x1 2.92 us: finish(): result.transpose(1, 0, 2).reshape(rows, heads * HEAD_DIM)]
    psum x1 -> x0, blocking collectives: 2.47 us -> none  [local(): row_sum, row_sq = lax.psum((row_sum, row_sq), 'mp')]
  transfers between devices with their start and end apart: 3 -> 0, of which waited for: 3 -> 0; matrix products, arithmetic and copies ran while one was open for 20% -> 0% of each run, Pallas kernels for 0% -> 0%
where the time goes in v1:
time: 74.4 us; the launch traced here: 73.9 us
  Pallas kernels  68.6 us (92%)
  local copies, waits for them, and re-layouts  3.9 us (5%)
  between operations  1.41 us (2%)
    pallas_call x1, Pallas kernels, fused(): pl.pallas_call(functools.partial(fused_kernel, n, mp_n, width), out_shape...  68.6 us
    unnamed x9, local copies, waits for them, and re-layouts  3.88 us

profile of v1, /device:TPU:0, one launch (start us, length us, event | category | flops | bytes accessed | tf_op | source)
XLA Modules:
  0.0 73.9 jit_solution(7021860884034083924)
XLA Ops:
  0.6 0.0 copy-start
  1.4 0.5 copy-done
  1.9 0.0 copy-start.1
  1.9 0.7 copy-done.1
  2.6 68.6 %shard_map.95 = (bf16[384,1536]{1,0:T(8,128)(2,1)S(1)}, bf16[384,1536]{1,0:T(8,128)(2,1)}) custom-call(bf16[192,3072]{1,0:T(8,128)(2,1)} %q_ref.1, bf16[192,3072]{1,0:T(8,128)(2,1)} %k_ref.1, bf16[192,3072]{1,0:T(8,128)(2,1)} %v_ref.1, s32[1,192]{1,0:T(1,128)S(1)} %bitcast.9, f32[3,1536]{1,0:T(4,128)S(1)} %bitcast.8, bf16[384,1536]{1,0:T(8,128)(2,1)} %res_ref.1, ...), custom_call_target="tpu_custom_call" | custom-call | tf_op jit(solution)/shard_map/pallas_call | solution.py:290
  71.2 0.0 copy-start.2
  71.2 1.0 %copy.16 = bf16[384,1536]{1,0:T(8,128)(2,1)} copy(bf16[384,1536]{1,0:T(8,128)(2,1)S(1)} %get-tuple-element.4) | data formatting | bytes 2359296
  72.2 0.7 copy-done.2
  72.9 1.0 %copy.17 = bf16[384,1536]{1,0:T(8,128)(2,1)} copy(bf16[384,1536]{1,0:T(8,128)(2,1)S(1)} %copy-done.2) | data formatting | bytes 2359296
  (2 shorter events, 0.0 us)
Async XLA Ops:
  0.6 1.2 %copy-start = (f32[50,3,1536]{2,0,1:T(8,128)S(1)}, f32[50,3,1536]{2,0,1:T(8,128)}, u32[]{:S(2)}) copy-start(f32[50,3,1536]{2,0,1:T(8,128)} %param.14) | copy-start | bytes 2764804
  1.9 0.7 copy-start.1
  71.2 1.7 %copy-start.2 = (bf16[384,1536]{1,0:T(8,128)(2,1)S(1)}, bf16[384,1536]{1,0:T(8,128)(2,1)}, u32[]{:S(2)}) copy-start(bf16[384,1536]{1,0:T(8,128)(2,1)} %get-tuple-element.5) | copy-start | bytes 3538948

commit v2 on v0

--- a/solution.py
+++ b/solution.py
@@ -1,9 +1,384 @@
+import functools
+import math
+
 import jax
 import jax.numpy as jnp
 from jax import lax
+from jax.experimental import pallas as pl
+from jax.experimental.pallas import tpu as pltpu
 from jax.sharding import PartitionSpec as P
 
 HEAD_DIM = 128
+VIDEOS = 4
+MESH = pl.DeviceIdType.MESH
+
+
+def rows_at(index, count):
+    return pl.ds(pl.multiple_of(index * count, count), count)
+
+
+def whole(ref, sem):
+    return pltpu.make_async_copy(ref, ref, sem)
+
+
+def fused_kernel(
+    n, mp_n,
+    q_ref, k_ref, v_ref, ids_ref, step_ref, mod_ref, res_ref, w_ref,
+    acc, stat_out, mod_out,
+    stage, qkv, weights, weight_sum, obuf, att, wbuf, res, mods, ids_mine, counts,
+    stat_mine, stat_other,
+    stage_sem, qkv_send, kq_recv, v_recv, o_send, o_recv, fwd_send, fwd_recv,
+    cnt_send, cnt_recv, stat_send, stat_recv, w_sem, in_sem,
+):
+    seq_i = lax.axis_index("seq")
+    mp_i = lax.axis_index("mp")
+    me = seq_i * mp_n + mp_i
+    rows = q_ref.shape[0]
+    groups = qkv.shape[0]
+    tokens = qkv.shape[2]
+    columns = w_ref.shape[1]
+    sibling = {"mp": 1 - mp_i}
+
+    def device(p):
+        return {"seq": lax.div(p, mp_n), "mp": lax.rem(p, mp_n)}
+
+    def each_peer(body):
+        def step(d, carry):
+            body(lax.rem(me + d, n))
+            return carry
+
+        lax.fori_loop(1, n, step, 0)
+
+    def every(body):
+        def step(p, carry):
+            body(p)
+            return carry
+
+        lax.fori_loop(0, n, step, 0)
+
+    sources = (k_ref, q_ref, v_ref)
+    slots = ((0, 1), (2,))
+
+    def part_recv(g, part):
+        return (kq_recv, v_recv)[part].at[g]
+
+    def load_part(g, part):
+        for t in slots[part]:
+
+            def load(p, t=t):
+                pltpu.make_async_copy(
+                    sources[t].at[:, rows_at(p * groups + g, HEAD_DIM)],
+                    stage.at[g, t, p],
+                    stage_sem.at[g, part],
+                ).start()
+
+            every(load)
+            pltpu.make_async_copy(
+                sources[t].at[:, rows_at(me * groups + g, HEAD_DIM)],
+                qkv.at[g, t, rows_at(me, rows)],
+                part_recv(g, part),
+            ).start()
+
+    def part_of(ref, g, part):
+        return ref.at[g, pl.ds(slots[part][0], len(slots[part]))]
+
+    def send_part(g, part):
+        whole(part_of(stage, g, part), stage_sem.at[g, part]).wait()
+        for t in slots[part]:
+
+            def send(p, t=t):
+                pltpu.make_async_remote_copy(
+                    src_ref=stage.at[g, t, p],
+                    dst_ref=qkv.at[g, t, rows_at(me, rows)],
+                    send_sem=qkv_send.at[g, part],
+                    recv_sem=part_recv(g, part),
+                    device_id=device(p),
+                    device_id_type=MESH,
+                ).start()
+
+            each_peer(send)
+
+    def wait_part(g, part):
+        whole(part_of(qkv, g, part), part_recv(g, part)).wait()
+
+    barrier = pltpu.get_barrier_semaphore()
+    each_peer(
+        lambda p: pl.semaphore_signal(
+            barrier, inc=1, device_id=device(p), device_id_type=MESH
+        )
+    )
+    load_part(0, 0)
+    load_part(0, 1)
+    load_ids = pltpu.make_async_copy(ids_ref, ids_mine, in_sem.at[0])
+    load_res = pltpu.make_async_copy(res_ref, res, in_sem.at[1])
+    load_mods = pltpu.make_async_copy(mod_ref, mods, in_sem.at[2])
+    load_ids.start()
+    for g in range(1, groups):
+        load_part(g, 0)
+        load_part(g, 1)
+    pl.semaphore_wait(barrier, n - 1)
+
+    order = [(g, part) for g in range(groups) for part in range(2)]
+    ahead = 3
+    for g, part in order[:ahead]:
+        send_part(g, part)
+
+    load_ids.wait()
+    ids = ids_mine[...]
+    below = [
+        jnp.sum((ids <= k).astype(jnp.float32), axis=1, keepdims=True)
+        for k in range(VIDEOS - 1)
+    ]
+    line = lax.broadcasted_iota(jnp.int32, (8, 128), 0)
+    mine = jnp.where(line == 0, below[0], jnp.where(line == 1, below[1], below[2]))
+    counts[rows_at(me, 8), :] = mine
+
+    def send_count(p):
+        pltpu.make_async_remote_copy(
+            src_ref=counts.at[rows_at(me, 8)],
+            dst_ref=counts.at[rows_at(me, 8)],
+            send_sem=cnt_send,
+            recv_sem=cnt_recv,
+            device_id=device(p),
+            device_id_type=MESH,
+        ).start()
+
+    each_peer(send_count)
+    load_res.start()
+    load_mods.start()
+    for g in range(groups):
+
+        def load_weight(p, g=g):
+            pltpu.make_async_copy(
+                w_ref.at[rows_at(p * groups + g, HEAD_DIM)],
+                wbuf.at[g, rows_at(p, HEAD_DIM)],
+                w_sem.at[g],
+            ).start()
+
+        every(load_weight)
+
+    whole(counts.at[pl.ds(0, 8 * (n - 1))], cnt_recv).wait()
+    sums = counts[pl.ds(0, 8), :]
+    for r in range(1, n):
+        sums = sums + counts[pl.ds(8 * r, 8), :]
+    totals = [sums[k : k + 1, 0:1] for k in range(VIDEOS - 1)]
+    factor = math.log2(math.e) / HEAD_DIM**0.5
+
+    def scores(g):
+        lane = lax.broadcasted_iota(jnp.int32, (1, tokens), 1).astype(jnp.float32)
+        key_ids = sum((lane >= c).astype(jnp.float32) for c in totals)
+
+        def step(p):
+            at = rows_at(p, rows)
+            place = (lax.broadcasted_iota(jnp.int32, (rows, 1), 0) + p * rows).astype(
+                jnp.float32
+            )
+            own_ids = sum((place >= c).astype(jnp.float32) for c in totals)
+            score = lax.dot_general(
+                qkv[g, 1, at, :],
+                qkv[g, 0],
+                (((1,), (1,)), ((), ())),
+                preferred_element_type=jnp.float32,
+            )
+            score = jnp.where(own_ids == key_ids, score, -1e30)
+            top = jnp.max(score, axis=1, keepdims=True)
+            weight = jnp.exp2((score - top) * factor)
+            total = jnp.sum(weight, axis=1, keepdims=True)
+            weights[at, :] = weight.astype(jnp.bfloat16)
+            weight_sum[at, :] = jnp.broadcast_to(total, (rows, HEAD_DIM))
+
+        every(step)
+
+    def attend_rows(g, p):
+        at = rows_at(p, rows)
+        summed = jnp.dot(
+            weights[at, :], qkv[g, 2], preferred_element_type=jnp.float32
+        )
+        obuf[g, at, :] = (summed / weight_sum[at, :]).astype(jnp.bfloat16)
+
+    def attend_and_send(g):
+        def send(p):
+            attend_rows(g, p)
+            pltpu.make_async_remote_copy(
+                src_ref=obuf.at[g, rows_at(p, rows)],
+                dst_ref=att.at[
+                    g, rows_at(lax.rem(p, mp_n), rows), rows_at(me, HEAD_DIM)
+                ],
+                send_sem=o_send.at[g],
+                recv_sem=o_recv.at[g, me],
+                device_id=device(p),
+                device_id_type=MESH,
+            ).start()
+
+        each_peer(send)
+        attend_rows(g, me)
+        pltpu.make_async_copy(
+            obuf.at[g, rows_at(me, rows)],
+            att.at[g, rows_at(mp_i, rows), rows_at(me, HEAD_DIM)],
+            o_recv.at[g, me],
+        ).start()
+
+    def pass_on(g):
+        def step(d, carry):
+            p = lax.rem(me + n - d, n)
+            block = att.at[g, rows_at(mp_i, rows), rows_at(p, HEAD_DIM)]
+            whole(block, o_recv.at[g, p]).wait()
+            pltpu.make_async_remote_copy(
+                src_ref=block,
+                dst_ref=block,
+                send_sem=fwd_send.at[g],
+                recv_sem=fwd_recv.at[g],
+                device_id=sibling,
+                device_id_type=MESH,
+            ).start()
+            return carry
+
+        lax.fori_loop(1, n + 1, step, 0)
+
+    def project(g, half):
+        rows_of = rows_at(half, rows)
+        tile = 2 * HEAD_DIM
+
+        def step(i, carry):
+            at = rows_at(i, tile)
+            part = jnp.dot(
+                att[g, rows_of, :], wbuf[g, :, at], preferred_element_type=jnp.float32
+            )
+            acc[rows_of, at] = part if g == 0 else acc[rows_of, at] + part
+            return carry
+
+        lax.fori_loop(0, columns // tile, step, 0)
+
+    def wait_forward(g):
+        whole(att.at[g, rows_at(1 - mp_i, rows)], fwd_recv.at[g]).wait()
+
+    def project_both(g):
+        whole(wbuf.at[g], w_sem.at[g]).wait()
+        wait_forward(g)
+        project(g, mp_i)
+        project(g, 1 - mp_i)
+
+    for g in range(groups):
+        for part in range(2):
+            wait_part(g, part)
+            later = 2 * g + part + ahead
+            if later < len(order):
+                send_part(*order[later])
+            if part == 0:
+                scores(g)
+        attend_and_send(g)
+        if g >= 1:
+            pass_on(g - 1)
+        if g >= 2:
+            project_both(g - 2)
+    if groups >= 2:
+        project_both(groups - 2)
+    last = groups - 1
+    pass_on(last)
+
+    load_res.wait()
+    load_mods.wait()
+    chosen = step_ref[0]
+    gate = mods[0, pl.ds(chosen, 1), :]
+    mod_out[0:1, :] = mods[1, pl.ds(chosen, 1), :]
+    mod_out[1:2, :] = mods[2, pl.ds(chosen, 1), :]
+    tile = rows // 3 if rows % 48 == 0 else 16
+    side = lax.broadcasted_iota(jnp.int32, (tile, 128), 1) < 64
+
+    def stats(half):
+        part = rows_at(half, rows)
+        return pltpu.make_async_remote_copy(
+            src_ref=stat_mine.at[part],
+            dst_ref=stat_other.at[part],
+            send_sem=stat_send.at[half],
+            recv_sem=stat_recv.at[half],
+            device_id=sibling,
+            device_id_type=MESH,
+        )
+
+    def finish(half):
+        project(last, half)
+
+        def gated(i, carry):
+            at = rows_at(half * (rows // tile) + i, tile)
+            stream = res[at, :].astype(jnp.float32) + gate * acc[at, :]
+            acc[at, :] = stream
+            row_sum = jnp.sum(stream, axis=1, keepdims=True)
+            row_sq = jnp.sum(stream * stream, axis=1, keepdims=True)
+            stat_mine[at, :] = jnp.where(side, row_sum, row_sq)
+            return carry
+
+        lax.fori_loop(0, rows // tile, gated, 0)
+        stats(half).start()
+
+    whole(wbuf.at[last], w_sem.at[last]).wait()
+    finish(mp_i)
+    wait_forward(last)
+    finish(1 - mp_i)
+
+    whole(counts.at[pl.ds(0, 8 * (n - 1))], cnt_send).wait()
+    for g in range(groups):
+        for part in range(2):
+            sent = part_of(qkv, g, part).at[:, pl.ds(0, rows * (n - 1))]
+            whole(sent, qkv_send.at[g, part]).wait()
+        whole(obuf.at[g, pl.ds(0, rows * (n - 1))], o_send.at[g]).wait()
+        whole(att.at[g, rows_at(mp_i, rows)], fwd_send.at[g]).wait()
+    for half in range(2):
+        stats(half).wait_recv()
+    stat_out[...] = stat_mine[...] + stat_other[...]
+    for half in range(2):
+        stats(half).wait_send()
+
+
+def fused(n, mp_n, residual, queries, keys, values, video_ids, timestep, modulation, out_weight):
+    rows, width = queries.shape
+    high, columns = residual.shape
+    tokens = rows * n
+    groups = width // HEAD_DIM // n
+    steps = modulation.shape[0]
+    bf16, f32 = jnp.bfloat16, jnp.float32
+    dma = pltpu.SemaphoreType.DMA
+    anywhere = pl.BlockSpec(memory_space=pl.ANY)
+    smem = pl.BlockSpec(memory_space=pltpu.SMEM)
+    vmem = pl.BlockSpec(memory_space=pltpu.VMEM)
+    stream, stat, mods = pl.pallas_call(
+        functools.partial(fused_kernel, n, mp_n),
+        out_shape=(
+            jax.ShapeDtypeStruct((high, columns), f32),
+            jax.ShapeDtypeStruct((high, 128), f32),
+            jax.ShapeDtypeStruct((2, columns), f32),
+        ),
+        in_specs=[anywhere, anywhere, anywhere, anywhere, smem, anywhere, anywhere, anywhere],
+        out_specs=(vmem, vmem, vmem),
+        scratch_shapes=[
+            pltpu.VMEM((groups, 3, n, rows, HEAD_DIM), bf16),
+            pltpu.VMEM((groups, 3, tokens, HEAD_DIM), bf16),
+            pltpu.VMEM((tokens, tokens), bf16),
+            pltpu.VMEM((tokens, HEAD_DIM), f32),
+            pltpu.VMEM((groups, tokens, HEAD_DIM), bf16),
+            pltpu.VMEM((groups, high, n * HEAD_DIM), bf16),
+            pltpu.VMEM((groups, n * HEAD_DIM, columns), bf16),
+            pltpu.VMEM((high, columns), bf16),
+            pltpu.VMEM((3, steps, columns), f32),
+            pltpu.VMEM((1, rows), jnp.int32),
+            pltpu.VMEM((8 * n, 128), f32),
+            pltpu.VMEM((high, 128), f32),
+            pltpu.VMEM((high, 128), f32),
+            dma((groups, 2)), dma((groups, 2)), dma((groups,)), dma((groups,)),
+            dma((groups,)), dma((groups, n)), dma((groups,)), dma((groups,)),
+            dma, dma, dma((2,)), dma((2,)), dma((groups,)), dma((3,)),
+        ],
+        compiler_params=pltpu.CompilerParams(
+            collective_id=0, has_side_effects=True, vmem_limit_bytes=52 * 2**20
+        ),
+    )(
+        queries, keys, values, video_ids.reshape(1, rows), timestep,
+        modulation.transpose(1, 0, 2), residual, out_weight,
+    )
+    mean = stat[:, 0:1] / width
+    var = stat[:, 64:65] / width - mean * mean
+    normed = (stream - mean) * lax.rsqrt(var + 1e-06) * (1.0 + mods[1:2]) + mods[0:1]
+    return (stream.astype(bf16), normed.astype(bf16))
 
 
 def attend(carry, q_rows, q_ids, key_rows, value_rows, key_ids):
@@ -101,9 +476,23 @@
     return (stream.astype(jnp.bfloat16), normed.astype(jnp.bfloat16))
 
 
+def choose(mesh):
+    seq_n, mp_n = mesh.shape["seq"], mesh.shape["mp"]
+    n = seq_n * mp_n
+
+    def run(*arrays):
+        queries = arrays[1]
+        rows, width = queries.shape
+        if mp_n == 2 and width // HEAD_DIM % n == 0 and rows % 64 == 0 and rows * n % 256 == 0:
+            return fused(n, mp_n, *arrays)
+        return local(*arrays)
+
+    return run
+
+
 def solution(mesh):
     return jax.shard_map(
-        local,
+        choose(mesh),
         mesh=mesh,
         in_specs=(
             P(("dp", "seq"), "mp"),

time: 207 us -> 78.1 us (0.38)
  waiting for transfers between devices: 83.5 us -> 0 us
  Pallas kernels: 0 us -> 70.1 us
  matrix products: 50.3 us -> 0 us
  local copies, waits for them, and re-layouts: 31.4 us -> 1.89 us
  between operations: 15.2 us -> 1.3 us
  blocking collectives: 12 us -> 0 us
  other arithmetic: 13.1 us -> 4.56 us
    all_gather x3 -> x0, waiting for transfers between devices: 82.1 us -> none  [the longest x1 48.5 us: local(): lax.all_gather(keys, ('seq', 'mp'), axis=0, tiled=True)]
    pallas_call x0 -> x1, Pallas kernels: none -> 70.1 us  [fused(): pl.pallas_call(functools.partial(fused_kernel, n, mp_n), out_shape=(jax.S...]
    dot_general x18 -> x0, matrix products: 50.3 us -> none  [the longest x8 24.2 us: attend(): jnp.einsum('thd,nhd->htn', q_heads[:, first:first + 3], k_heads[:, first:...]
    all_gather x2 -> x0, local copies, waits for them, and re-layouts: 25.5 us -> none  [the longest x1 12.8 us: local(): lax.all_gather(keys, ('seq', 'mp'), axis=0, tiled=True)]
    unnamed x1 -> x0, blocking collectives: 9.55 us -> none
    reduce_sum x1 -> x0, other arithmetic: 7.82 us -> none  [attend(): new_total.append(jnp.sum(weight, axis=2))]
    psum x1 -> x0, blocking collectives: 2.47 us -> none  [local(): row_sum, row_sq = lax.psum((row_sum, row_sq), 'mp')]
    unnamed x30 -> x4, local copies, waits for them, and re-layouts: 4.25 us -> 1.89 us
  transfers between devices with their start and end apart: 3 -> 0, of which waited for: 3 -> 0; matrix products, arithmetic and copies ran while one was open for 20% -> 0% of each run, Pallas kernels for 0% -> 0%
where the time goes in v2:
time: 78.1 us; the launch traced here: 77.9 us
  Pallas kernels  70.1 us (90%)
  other arithmetic  4.56 us (6%)
  local copies, waits for them, and re-layouts  1.89 us (2%)
  between operations  1.3 us (2%)
    pallas_call x1, Pallas kernels, fused(): pl.pallas_call(functools.partial(fused_kernel, n, mp_n), out_shape=(jax.S...  70.1 us
    convert_element_type x1, other arithmetic, fused(): return (stream.astype(bf16), normed.astype(bf16))  4.28 us
    unnamed x4, local copies, waits for them, and re-layouts  1.89 us

profile of v2, /device:TPU:0, one launch (start us, length us, event | category | flops | bytes accessed | tf_op | source)
XLA Modules:
  0.0 77.9 jit_solution(14607750260128088738)
XLA Ops:
  1.3 0.0 copy-start
  1.3 1.2 %copy-done = f32[50,3,1536]{2,0,1:T(8,128)S(1)} copy-done((f32[50,3,1536]{2,0,1:T(8,128)S(1)}, f32[50,3,1536]{2,0,1:T(8,128)}, u32[]{:S(2)}) %copy-start) | copy-done | bytes 921624
  2.5 0.0 copy-start.1
  2.5 0.7 copy-done.1
  3.2 70.1 %shard_map.95 = (f32[384,1536]{1,0:T(8,128)}, f32[384,128]{1,0:T(8,128)S(1)}, f32[2,1536]{1,0:T(2,128)S(1)}) custom-call(bf16[192,3072]{1,0:T(8,128)(2,1)} %q_ref.1, bf16[192,3072]{1,0:T(8,128)(2,1)} %k_ref.1, bf16[192,3072]{1,0:T(8,128)(2,1)} %v_ref.1, s32[1,192]{1,0:T(1,128)S(1)} %bitcast.3, s32[1]{0:T(128)S(6)} %copy.10.step_ref, ...), custom_call_target="tpu_custom_call" | custom-call | tf_op jit(solution)/shard_map/pallas_call | solution.py:344
  73.3 0.3 fusion
  73.6 4.3 %add_convert_fusion = (bf16[384,1536]{1,0:T(8,128)(2,1)}, bf16[384,1536]{1,0:T(8,128)(2,1)}) fusion(f32[384,1536]{1,0:T(8,128)} %get-tuple-element.5, f32[1536]{0:T(1024)S(1)} %get-tuple-element.11, f32[1536]{0:T(1024)S(1)} %get-tuple-element.10, f32[384]{0:T(512)S(1)} %get-tuple-element.9, f32[384]{0:T(512)S(1)} %get-tuple-element.8), kind=kLoop, calls=%fused_computation | loop fusion | flops 3538944 | bytes 4733952 | tf_op jit(solution)/shard_map/convert_element_type | solution.py:381
  (1 shorter events, 0.0 us)
Async XLA Ops:
  1.3 1.2 %copy-start = (f32[50,3,1536]{2,0,1:T(8,128)S(1)}, f32[50,3,1536]{2,0,1:T(8,128)}, u32[]{:S(2)}) copy-start(f32[50,3,1536]{2,0,1:T(8,128)} %param.14) | copy-start | bytes 2764804
  2.5 0.7 copy-start.1

commit v3 on v2

--- a/solution.py
+++ b/solution.py
@@ -1,5 +1,4 @@
 import functools
-import math
 
 import jax
 import jax.numpy as jnp
@@ -10,6 +9,7 @@
 
 HEAD_DIM = 128
 VIDEOS = 4
+MARK = 2.0**50
 MESH = pl.DeviceIdType.MESH
 
 
@@ -24,11 +24,11 @@
 def fused_kernel(
     n, mp_n,
     q_ref, k_ref, v_ref, ids_ref, step_ref, mod_ref, res_ref, w_ref,
-    acc, stat_out, mod_out,
-    stage, qkv, weights, weight_sum, obuf, att, wbuf, res, mods, ids_mine, counts,
+    stream_ref, stat_out, mod_out,
+    acc, stage, qkv, key_marks, query_marks, values_t, obuf, att, wbuf, res, mods, ids_mine, counts,
     stat_mine, stat_other,
     stage_sem, qkv_send, kq_recv, v_recv, o_send, o_recv, fwd_send, fwd_recv,
-    cnt_send, cnt_recv, stat_send, stat_recv, w_sem, in_sem,
+    cnt_send, cnt_recv, stat_send, stat_recv, w_sem, in_sem, out_sem,
 ):
     seq_i = lax.axis_index("seq")
     mp_i = lax.axis_index("mp")
@@ -162,61 +162,74 @@
     for r in range(1, n):
         sums = sums + counts[pl.ds(8 * r, 8), :]
     totals = [sums[k : k + 1, 0:1] for k in range(VIDEOS - 1)]
-    factor = math.log2(math.e) / HEAD_DIM**0.5
-
-    def scores(g):
-        lane = lax.broadcasted_iota(jnp.int32, (1, tokens), 1).astype(jnp.float32)
-        key_ids = sum((lane >= c).astype(jnp.float32) for c in totals)
-
-        def step(p):
-            at = rows_at(p, rows)
-            place = (lax.broadcasted_iota(jnp.int32, (rows, 1), 0) + p * rows).astype(
-                jnp.float32
-            )
-            own_ids = sum((place >= c).astype(jnp.float32) for c in totals)
-            score = lax.dot_general(
-                qkv[g, 1, at, :],
-                qkv[g, 0],
-                (((1,), (1,)), ((), ())),
-                preferred_element_type=jnp.float32,
-            )
-            score = jnp.where(own_ids == key_ids, score, -1e30)
-            top = jnp.max(score, axis=1, keepdims=True)
-            weight = jnp.exp2((score - top) * factor)
-            total = jnp.sum(weight, axis=1, keepdims=True)
-            weights[at, :] = weight.astype(jnp.bfloat16)
-            weight_sum[at, :] = jnp.broadcast_to(total, (rows, HEAD_DIM))
-
-        every(step)
-
-    def attend_rows(g, p):
-        at = rows_at(p, rows)
-        summed = jnp.dot(
-            weights[at, :], qkv[g, 2], preferred_element_type=jnp.float32
-        )
-        obuf[g, at, :] = (summed / weight_sum[at, :]).astype(jnp.bfloat16)
+    tile = 2 * HEAD_DIM
+
+    def mark(i, carry):
+        at = rows_at(i, tile)
+        place = (lax.broadcasted_iota(jnp.int32, (tile, 1), 0) + i * tile).astype(
+            jnp.float32
+        )
+        own = sum((place >= c).astype(jnp.float32) for c in totals)
+        video = lax.broadcasted_iota(jnp.int32, (tile, HEAD_DIM), 1).astype(jnp.float32)
+        key_marks[at, :] = jnp.where(own == video, -MARK, 0.0).astype(jnp.bfloat16)
+        other = jnp.where(own == video, 0.0, MARK)
+        query_marks[at, :] = jnp.where(video < VIDEOS, other, 0.0).astype(jnp.bfloat16)
+        return carry
+
+    lax.fori_loop(0, tokens // tile, mark, 0)
+    values_t[HEAD_DIM:, :] = jnp.ones((values_t.shape[0] - HEAD_DIM, tokens), jnp.bfloat16)
+    chunk = tokens // 2
+    peers = n // 2
+
+    def attend_tile(g, start):
+        at = pl.ds(pl.multiple_of(start, tile), tile)
+        score = lax.dot_general(
+            jnp.concatenate([qkv[g, 0], key_marks[...]], axis=1),
+            jnp.concatenate([qkv[g, 1, at, :], query_marks[at, :]], axis=1),
+            (((1,), (1,)), ((), ())),
+            preferred_element_type=jnp.float32,
+        )
+        top = jnp.max(score, axis=0, keepdims=True)
+        weight = jnp.exp((score - top) * (1.0 / HEAD_DIM**0.5)).astype(jnp.bfloat16)
+        summed = jnp.dot(values_t[...], weight, preferred_element_type=jnp.float32)
+        result = summed[:HEAD_DIM] / summed[HEAD_DIM : HEAD_DIM + 1]
+        obuf[g, at, :] = result.T.astype(jnp.bfloat16)
 
     def attend_and_send(g):
-        def send(p):
-            attend_rows(g, p)
-            pltpu.make_async_remote_copy(
-                src_ref=obuf.at[g, rows_at(p, rows)],
-                dst_ref=att.at[
+        values_t[:HEAD_DIM, :] = qkv[g, 2].T
+
+        def half(j, carry):
+            part = lax.rem(lax.div(me, peers) + 1 + j, 2)
+            for i in range(chunk // tile):
+                attend_tile(g, part * chunk + i * tile)
+
+            def send(d, carry):
+                p = part * peers + lax.rem(me + d, peers)
+                block = obuf.at[g, rows_at(p, rows)]
+                there = att.at[
                     g, rows_at(lax.rem(p, mp_n), rows), rows_at(me, HEAD_DIM)
-                ],
-                send_sem=o_send.at[g],
-                recv_sem=o_recv.at[g, me],
-                device_id=device(p),
-                device_id_type=MESH,
-            ).start()
-
-        each_peer(send)
-        attend_rows(g, me)
-        pltpu.make_async_copy(
-            obuf.at[g, rows_at(me, rows)],
-            att.at[g, rows_at(mp_i, rows), rows_at(me, HEAD_DIM)],
-            o_recv.at[g, me],
-        ).start()
+                ]
+
+                @pl.when(p != me)
+                def _():
+                    pltpu.make_async_remote_copy(
+                        src_ref=block,
+                        dst_ref=there,
+                        send_sem=o_send.at[g],
+                        recv_sem=o_recv.at[g, me],
+                        device_id=device(p),
+                        device_id_type=MESH,
+                    ).start()
+
+                @pl.when(p == me)
+                def _():
+                    pltpu.make_async_copy(block, there, o_recv.at[g, me]).start()
+
+                return carry
+
+            return lax.fori_loop(0, peers, send, carry)
+
+        lax.fori_loop(0, 2, half, 0)
 
     def pass_on(g):
         def step(d, carry):
@@ -264,8 +277,6 @@
             later = 2 * g + part + ahead
             if later < len(order):
                 send_part(*order[later])
-            if part == 0:
-                scores(g)
         attend_and_send(g)
         if g >= 1:
             pass_on(g - 1)
@@ -296,6 +307,10 @@
             device_id_type=MESH,
         )
 
+    def store(half):
+        part = rows_at(half, rows)
+        return pltpu.make_async_copy(acc.at[part], stream_ref.at[part], out_sem.at[half])
+
     def finish(half):
         project(last, half)
 
@@ -310,6 +325,7 @@
 
         lax.fori_loop(0, rows // tile, gated, 0)
         stats(half).start()
+        store(half).start()
 
     whole(wbuf.at[last], w_sem.at[last]).wait()
     finish(mp_i)
@@ -328,6 +344,46 @@
     stat_out[...] = stat_mine[...] + stat_other[...]
     for half in range(2):
         stats(half).wait_send()
+        store(half).wait()
+
+
+def norm_kernel(
+    width, stream_ref, stat_ref, mod_ref, hid_ref, mlp_ref,
+    stream_in, stat, mod, hid, mlp, load_sems, sems,
+):
+    tile = 64
+    count = stream_ref.shape[0] // tile
+    load_mod = pltpu.make_async_copy(mod_ref, mod, load_sems.at[count])
+    load_stat = pltpu.make_async_copy(stat_ref, stat, load_sems.at[count + 1])
+    load_mod.start()
+    load_stat.start()
+    loads = []
+    for i in range(count):
+        at = pl.ds(i * tile, tile)
+        loads.append(
+            pltpu.make_async_copy(stream_ref.at[at], stream_in.at[at], load_sems.at[i])
+        )
+        loads[i].start()
+    load_mod.wait()
+    load_stat.wait()
+    shift = mod[0:1, :]
+    scale = 1.0 + mod[1:2, :]
+    copies = []
+    for i in range(count):
+        at = pl.ds(i * tile, tile)
+        loads[i].wait()
+        stream = stream_in[at, :]
+        mean = stat[at, 0:1] / width
+        var = stat[at, 64:65] / width - mean * mean
+        hid[at, :] = stream.astype(jnp.bfloat16)
+        result = (stream - mean) * lax.rsqrt(var + 1e-06) * scale + shift
+        mlp[at, :] = result.astype(jnp.bfloat16)
+        for k, (source, target) in enumerate(((hid, hid_ref), (mlp, mlp_ref))):
+            copy = pltpu.make_async_copy(source.at[at], target.at[at], sems.at[k, i])
+            copy.start()
+            copies.append(copy)
+    for copy in copies:
+        copy.wait()
 
 
 def fused(n, mp_n, residual, queries, keys, values, video_ids, timestep, modulation, out_weight):
@@ -338,7 +394,7 @@
     steps = modulation.shape[0]
     bf16, f32 = jnp.bfloat16, jnp.float32
     dma = pltpu.SemaphoreType.DMA
-    anywhere = pl.BlockSpec(memory_space=pl.ANY)
+    hbm = pl.BlockSpec(memory_space=pltpu.HBM)
     smem = pl.BlockSpec(memory_space=pltpu.SMEM)
     vmem = pl.BlockSpec(memory_space=pltpu.VMEM)
     stream, stat, mods = pl.pallas_call(
@@ -348,13 +404,15 @@
             jax.ShapeDtypeStruct((high, 128), f32),
             jax.ShapeDtypeStruct((2, columns), f32),
         ),
-        in_specs=[anywhere, anywhere, anywhere, anywhere, smem, anywhere, anywhere, anywhere],
-        out_specs=(vmem, vmem, vmem),
+        in_specs=[hbm, hbm, hbm, hbm, smem, hbm, hbm, hbm],
+        out_specs=(hbm, vmem, vmem),
         scratch_shapes=[
+            pltpu.VMEM((high, columns), f32),
             pltpu.VMEM((groups, 3, n, rows, HEAD_DIM), bf16),
             pltpu.VMEM((groups, 3, tokens, HEAD_DIM), bf16),
-            pltpu.VMEM((tokens, tokens), bf16),
-            pltpu.VMEM((tokens, HEAD_DIM), f32),
+            pltpu.VMEM((tokens, HEAD_DIM), bf16),
+            pltpu.VMEM((tokens, HEAD_DIM), bf16),
+            pltpu.VMEM((HEAD_DIM + 16, tokens), bf16),
             pltpu.VMEM((groups, tokens, HEAD_DIM), bf16),
             pltpu.VMEM((groups, high, n * HEAD_DIM), bf16),
             pltpu.VMEM((groups, n * HEAD_DIM, columns), bf16),
@@ -367,18 +425,32 @@
             dma((groups, 2)), dma((groups, 2)), dma((groups,)), dma((groups,)),
             dma((groups,)), dma((groups, n)), dma((groups,)), dma((groups,)),
             dma, dma, dma((2,)), dma((2,)), dma((groups,)), dma((3,)),
+            dma((2,)),
         ],
         compiler_params=pltpu.CompilerParams(
-            collective_id=0, has_side_effects=True, vmem_limit_bytes=52 * 2**20
+            collective_id=0, has_side_effects=True, vmem_limit_bytes=56 * 2**20
         ),
     )(
         queries, keys, values, video_ids.reshape(1, rows), timestep,
         modulation.transpose(1, 0, 2), residual, out_weight,
     )
-    mean = stat[:, 0:1] / width
-    var = stat[:, 64:65] / width - mean * mean
-    normed = (stream - mean) * lax.rsqrt(var + 1e-06) * (1.0 + mods[1:2]) + mods[0:1]
-    return (stream.astype(bf16), normed.astype(bf16))
+    out = jax.ShapeDtypeStruct(residual.shape, bf16)
+    return pl.pallas_call(
+        functools.partial(norm_kernel, width),
+        out_shape=(out, out),
+        in_specs=[hbm, hbm, hbm],
+        out_specs=(hbm, hbm),
+        scratch_shapes=[
+            pltpu.VMEM((high, columns), f32),
+            pltpu.VMEM((high, 128), f32),
+            pltpu.VMEM((2, columns), f32),
+            pltpu.VMEM((high, columns), bf16),
+            pltpu.VMEM((high, columns), bf16),
+            dma((high // 64 + 2,)),
+            dma((2, high // 64)),
+        ],
+        compiler_params=pltpu.CompilerParams(vmem_limit_bytes=56 * 2**20),
+    )(stream, stat, mods)
 
 
 def attend(carry, q_rows, q_ids, key_rows, value_rows, key_ids):
@@ -483,7 +555,7 @@
     def run(*arrays):
         queries = arrays[1]
         rows, width = queries.shape
-        if mp_n == 2 and width // HEAD_DIM % n == 0 and rows % 64 == 0 and rows * n % 256 == 0:
+        if mp_n == 2 and width // HEAD_DIM % n == 0 and rows % 64 == 0 and rows * n % 512 == 0:
             return fused(n, mp_n, *arrays)
         return local(*arrays)
 

time: 78.1 us -> 76.7 us (0.982)
  other arithmetic: 4.56 us -> 0 us
  Pallas kernels: 70.1 us -> 74.6 us
  local copies, waits for them, and re-layouts: 1.89 us -> 0 us
    convert_element_type x1 -> x0, other arithmetic: 4.28 us -> none  [fused(): return (stream.astype(bf16), normed.astype(bf16))]
    pallas_call x0 -> x1, Pallas kernels: none -> 3.2 us  [fused(): pl.pallas_call(functools.partial(norm_kernel, width), out_shape=(out, out...]
    unnamed x4 -> x0, local copies, waits for them, and re-layouts: 1.89 us -> none
    pallas_call x1, Pallas kernels: 70.1 us -> 71.4 us  [fused(): pl.pallas_call(functools.partial(fused_kernel, n, mp_n), out_shape=(jax.S...]
where the time goes in v3:
time: 76.7 us; the launch traced here: 75.9 us
  Pallas kernels  74.6 us (97%)
  between operations  1.29 us (2%)
    pallas_call x1, Pallas kernels, fused(): pl.pallas_call(functools.partial(fused_kernel, n, mp_n), out_shape=(jax.S...  71.4 us
    pallas_call x1, Pallas kernels, fused(): pl.pallas_call(functools.partial(norm_kernel, width), out_shape=(out, out...  3.2 us

profile of v3, /device:TPU:0, one launch (start us, length us, event | category | flops | bytes accessed | tf_op | source)
XLA Modules:
  0.0 75.9 jit_solution(15016317761092473744)
XLA Ops:
  1.3 71.4 %shard_map.95 = (f32[384,1536]{1,0:T(8,128)}, f32[384,128]{1,0:T(8,128)}, f32[2,1536]{1,0:T(2,128)}) custom-call(bf16[192,3072]{1,0:T(8,128)(2,1)} %q_ref.1, bf16[192,3072]{1,0:T(8,128)(2,1)} %k_ref.1, bf16[192,3072]{1,0:T(8,128)(2,1)} %v_ref.1, s32[1,192]{1,0:T(1,128)} %bitcast.3, s32[1]{0:T(128)S(6)} %copy.10.step_ref, f32[3,50,1536]{2,1,0:T(8,128)} %bitcast.2, ...), custom_call_target="tpu_custom_call" | custom-call | tf_op jit(solution)/shard_map/pallas_call | solution.py:400
  72.7 3.2 %shard_map.96 = (bf16[384,1536]{1,0:T(8,128)(2,1)}, bf16[384,1536]{1,0:T(8,128)(2,1)}) custom-call(f32[384,1536]{1,0:T(8,128)} %get-tuple-element.5.stream_ref, f32[384,128]{1,0:T(8,128)} %get-tuple-element.6.stat_ref, f32[2,1536]{1,0:T(2,128)} %get-tuple-element.7.mod_ref), custom_call_target="tpu_custom_call" | custom-call | tf_op jit(solution)/shard_map/pallas_call | solution.py:438

commit v4 on v3

--- a/solution.py
+++ b/solution.py
@@ -25,22 +25,29 @@
     n, mp_n,
     q_ref, k_ref, v_ref, ids_ref, step_ref, mod_ref, res_ref, w_ref,
     stream_ref, stat_out, mod_out,
-    acc, stage, qkv, key_marks, query_marks, values_t, obuf, att, wbuf, res, mods, ids_mine, counts,
-    stat_mine, stat_other,
-    stage_sem, qkv_send, kq_recv, v_recv, o_send, o_recv, fwd_send, fwd_recv,
+    acc, keys_values, queries, key_marks, query_marks, values_t, obuf, att, wbuf, res,
+    mods, ids_mine, counts, stat_mine, stat_other,
+    x_send, kv_recv, q_recv, y_send, y_recv, o_send, o_recv, fwd_send, fwd_recv,
     cnt_send, cnt_recv, stat_send, stat_recv, w_sem, in_sem, out_sem,
 ):
     seq_i = lax.axis_index("seq")
     mp_i = lax.axis_index("mp")
     me = seq_i * mp_n + mp_i
+    row_n = n // 2
+    my_y = lax.div(me, row_n)
+    mine = lax.rem(me, row_n)
     rows = q_ref.shape[0]
-    groups = qkv.shape[0]
-    tokens = qkv.shape[2]
+    groups, half_tokens = queries.shape[0], queries.shape[1]
+    tokens = 2 * half_tokens
     columns = w_ref.shape[1]
     sibling = {"mp": 1 - mp_i}
+    opposite = {"seq": lax.rem(seq_i + row_n // mp_n, n // mp_n)}
 
     def device(p):
         return {"seq": lax.div(p, mp_n), "mp": lax.rem(p, mp_n)}
+
+    def in_row(r):
+        return device(my_y * row_n + r)
 
     def each_peer(body):
         def step(d, carry):
@@ -49,57 +56,59 @@
 
         lax.fori_loop(1, n, step, 0)
 
-    def every(body):
-        def step(p, carry):
-            body(p)
+    def row_peers(body):
+        def step(d, carry):
+            body(lax.rem(mine + d, row_n))
             return carry
 
-        lax.fori_loop(0, n, step, 0)
-
-    sources = (k_ref, q_ref, v_ref)
-    slots = ((0, 1), (2,))
-
-    def part_recv(g, part):
-        return (kq_recv, v_recv)[part].at[g]
-
-    def load_part(g, part):
-        for t in slots[part]:
-
-            def load(p, t=t):
-                pltpu.make_async_copy(
-                    sources[t].at[:, rows_at(p * groups + g, HEAD_DIM)],
-                    stage.at[g, t, p],
-                    stage_sem.at[g, part],
-                ).start()
-
-            every(load)
-            pltpu.make_async_copy(
-                sources[t].at[:, rows_at(me * groups + g, HEAD_DIM)],
-                qkv.at[g, t, rows_at(me, rows)],
-                part_recv(g, part),
-            ).start()
-
-    def part_of(ref, g, part):
-        return ref.at[g, pl.ds(slots[part][0], len(slots[part]))]
-
-    def send_part(g, part):
-        whole(part_of(stage, g, part), stage_sem.at[g, part]).wait()
-        for t in slots[part]:
-
-            def send(p, t=t):
+        lax.fori_loop(1, row_n, step, 0)
+
+    def head(r, g):
+        return rows_at(r * groups + g, HEAD_DIM)
+
+    def own_block(r):
+        return rows_at(my_y * row_n + r, rows)
+
+    def send_row(g):
+        for t, ref in enumerate((k_ref, v_ref, q_ref)):
+            if t < 2:
+                there, sem = keys_values.at[g, t, own_block(mine)], kv_recv.at[g, mine]
+            else:
+                there, sem = queries.at[g, rows_at(mine, rows)], q_recv.at[g]
+
+            def send(r, ref=ref, there=there, sem=sem):
                 pltpu.make_async_remote_copy(
-                    src_ref=stage.at[g, t, p],
-                    dst_ref=qkv.at[g, t, rows_at(me, rows)],
-                    send_sem=qkv_send.at[g, part],
-                    recv_sem=part_recv(g, part),
-                    device_id=device(p),
+                    src_ref=ref.at[:, head(r, g)],
+                    dst_ref=there,
+                    send_sem=x_send.at[g],
+                    recv_sem=sem,
+                    device_id=in_row(r),
                     device_id_type=MESH,
                 ).start()
 
-            each_peer(send)
-
-    def wait_part(g, part):
-        whole(part_of(qkv, g, part), part_recv(g, part)).wait()
+            pltpu.make_async_copy(ref.at[:, head(mine, g)], there, sem).start()
+            row_peers(send)
+
+    def send_across(g, r):
+        block = keys_values.at[g, :, own_block(r)]
+        whole(block, kv_recv.at[g, r]).wait()
+        pltpu.make_async_remote_copy(
+            src_ref=block,
+            dst_ref=block,
+            send_sem=y_send.at[g],
+            recv_sem=y_recv.at[g],
+            device_id=opposite,
+            device_id_type=MESH,
+        ).start()
+
+    def across_near(g):
+        send_across(g, mine)
+        send_across(g, mine + 1 - 2 * mp_i)
+
+    def across_far(g):
+        first = lax.rem(lax.div(mine, mp_n) + 1, row_n // mp_n) * mp_n
+        for core in range(mp_n):
+            send_across(g, first + core)
 
     barrier = pltpu.get_barrier_semaphore()
     each_peer(
@@ -107,21 +116,15 @@
             barrier, inc=1, device_id=device(p), device_id_type=MESH
         )
     )
-    load_part(0, 0)
-    load_part(0, 1)
     load_ids = pltpu.make_async_copy(ids_ref, ids_mine, in_sem.at[0])
     load_res = pltpu.make_async_copy(res_ref, res, in_sem.at[1])
     load_mods = pltpu.make_async_copy(mod_ref, mods, in_sem.at[2])
     load_ids.start()
-    for g in range(1, groups):
-        load_part(g, 0)
-        load_part(g, 1)
     pl.semaphore_wait(barrier, n - 1)
 
-    order = [(g, part) for g in range(groups) for part in range(2)]
     ahead = 3
-    for g, part in order[:ahead]:
-        send_part(g, part)
+    for g in range(ahead):
+        send_row(g)
 
     load_ids.wait()
     ids = ids_mine[...]
@@ -130,8 +133,9 @@
         for k in range(VIDEOS - 1)
     ]
     line = lax.broadcasted_iota(jnp.int32, (8, 128), 0)
-    mine = jnp.where(line == 0, below[0], jnp.where(line == 1, below[1], below[2]))
-    counts[rows_at(me, 8), :] = mine
+    counts[rows_at(me, 8), :] = jnp.where(
+        line == 0, below[0], jnp.where(line == 1, below[1], below[2])
+    )
 
     def send_count(p):
         pltpu.make_async_remote_copy(
@@ -144,18 +148,20 @@
         ).start()
 
     each_peer(send_count)
+    across_near(0)
+    across_near(1)
     load_res.start()
     load_mods.start()
-    for g in range(groups):
-
-        def load_weight(p, g=g):
-            pltpu.make_async_copy(
-                w_ref.at[rows_at(p * groups + g, HEAD_DIM)],
-                wbuf.at[g, rows_at(p, HEAD_DIM)],
-                w_sem.at[g],
-            ).start()
-
-        every(load_weight)
+
+    def load_weight(i, carry):
+        g, r = lax.div(i, row_n), lax.rem(i, row_n)
+        pltpu.make_async_copy(
+            w_ref.at[head(r, g)], wbuf.at[g, rows_at(r, HEAD_DIM)], w_sem.at[g]
+        ).start()
+        return carry
+
+    lax.fori_loop(0, groups * row_n, load_weight, 0)
+    acc[...] = jnp.zeros_like(acc)
 
     whole(counts.at[pl.ds(0, 8 * (n - 1))], cnt_recv).wait()
     sums = counts[pl.ds(0, 8), :]
@@ -178,64 +184,49 @@
 
     lax.fori_loop(0, tokens // tile, mark, 0)
     values_t[HEAD_DIM:, :] = jnp.ones((values_t.shape[0] - HEAD_DIM, tokens), jnp.bfloat16)
-    chunk = tokens // 2
-    peers = n // 2
-
-    def attend_tile(g, start):
-        at = pl.ds(pl.multiple_of(start, tile), tile)
-        score = lax.dot_general(
-            jnp.concatenate([qkv[g, 0], key_marks[...]], axis=1),
-            jnp.concatenate([qkv[g, 1, at, :], query_marks[at, :]], axis=1),
-            (((1,), (1,)), ((), ())),
-            preferred_element_type=jnp.float32,
-        )
-        top = jnp.max(score, axis=0, keepdims=True)
-        weight = jnp.exp((score - top) * (1.0 / HEAD_DIM**0.5)).astype(jnp.bfloat16)
-        summed = jnp.dot(values_t[...], weight, preferred_element_type=jnp.float32)
-        result = summed[:HEAD_DIM] / summed[HEAD_DIM : HEAD_DIM + 1]
-        obuf[g, at, :] = result.T.astype(jnp.bfloat16)
-
-    def attend_and_send(g):
-        values_t[:HEAD_DIM, :] = qkv[g, 2].T
-
-        def half(j, carry):
-            part = lax.rem(lax.div(me, peers) + 1 + j, 2)
-            for i in range(chunk // tile):
-                attend_tile(g, part * chunk + i * tile)
-
-            def send(d, carry):
-                p = part * peers + lax.rem(me + d, peers)
-                block = obuf.at[g, rows_at(p, rows)]
-                there = att.at[
-                    g, rows_at(lax.rem(p, mp_n), rows), rows_at(me, HEAD_DIM)
-                ]
-
-                @pl.when(p != me)
-                def _():
-                    pltpu.make_async_remote_copy(
-                        src_ref=block,
-                        dst_ref=there,
-                        send_sem=o_send.at[g],
-                        recv_sem=o_recv.at[g, me],
-                        device_id=device(p),
-                        device_id_type=MESH,
-                    ).start()
-
-                @pl.when(p == me)
-                def _():
-                    pltpu.make_async_copy(block, there, o_recv.at[g, me]).start()
-
-                return carry
-
-            return lax.fori_loop(0, peers, send, carry)
-
-        lax.fori_loop(0, 2, half, 0)
+    across_far(0)
+
+    def attention(g):
+        values_t[:HEAD_DIM, :] = keys_values[g, 1].T
+        for i in range(half_tokens // tile):
+            at = pl.ds(i * tile, tile)
+            marks = pl.ds(pl.multiple_of(my_y * half_tokens + i * tile, tile), tile)
+            score = lax.dot_general(
+                jnp.concatenate([keys_values[g, 0], key_marks[...]], axis=1),
+                jnp.concatenate([queries[g, at, :], query_marks[marks, :]], axis=1),
+                (((1,), (1,)), ((), ())),
+                preferred_element_type=jnp.float32,
+            )
+            top = jnp.max(score, axis=0, keepdims=True)
+            weight = jnp.exp((score - top) * (1.0 / HEAD_DIM**0.5)).astype(jnp.bfloat16)
+            summed = jnp.dot(values_t[...], weight, preferred_element_type=jnp.float32)
+            result = summed[:HEAD_DIM] / summed[HEAD_DIM : HEAD_DIM + 1]
+            obuf[g, at, :] = result.T.astype(jnp.bfloat16)
+
+    def send_back(g):
+        def landing(r):
+            return att.at[g, rows_at(lax.rem(r, mp_n), rows), rows_at(mine, HEAD_DIM)]
+
+        def send(r):
+            pltpu.make_async_remote_copy(
+                src_ref=obuf.at[g, rows_at(r, rows)],
+                dst_ref=landing(r),
+                send_sem=o_send.at[g],
+                recv_sem=o_recv.at[g, mine],
+                device_id=in_row(r),
+                device_id_type=MESH,
+            ).start()
+
+        row_peers(send)
+        pltpu.make_async_copy(
+            obuf.at[g, rows_at(mine, rows)], landing(mine), o_recv.at[g, mine]
+        ).start()
 
     def pass_on(g):
         def step(d, carry):
-            p = lax.rem(me + n - d, n)
-            block = att.at[g, rows_at(mp_i, rows), rows_at(p, HEAD_DIM)]
-            whole(block, o_recv.at[g, p]).wait()
+            r = lax.rem(mine + d, row_n)
+            block = att.at[g, rows_at(mp_i, rows), rows_at(r, HEAD_DIM)]
+            whole(block, o_recv.at[g, r]).wait()
             pltpu.make_async_remote_copy(
                 src_ref=block,
                 dst_ref=block,
@@ -246,18 +237,16 @@
             ).start()
             return carry
 
-        lax.fori_loop(1, n + 1, step, 0)
+        lax.fori_loop(0, row_n, step, 0)
 
     def project(g, half):
         rows_of = rows_at(half, rows)
-        tile = 2 * HEAD_DIM
 
         def step(i, carry):
             at = rows_at(i, tile)
-            part = jnp.dot(
+            acc[rows_of, at] += jnp.dot(
                 att[g, rows_of, :], wbuf[g, :, at], preferred_element_type=jnp.float32
             )
-            acc[rows_of, at] = part if g == 0 else acc[rows_of, at] + part
             return carry
 
         lax.fori_loop(0, columns // tile, step, 0)
@@ -271,20 +260,38 @@
         project(g, mp_i)
         project(g, 1 - mp_i)
 
-    for g in range(groups):
-        for part in range(2):
-            wait_part(g, part)
-            later = 2 * g + part + ahead
-            if later < len(order):
-                send_part(*order[later])
-        attend_and_send(g)
-        if g >= 1:
+    def group(g, carry):
+        @pl.when(g + ahead < groups)
+        def _():
+            send_row(g + ahead)
+
+        @pl.when(g + 2 < groups)
+        def _():
+            across_near(g + 2)
+
+        @pl.when(g + 1 < groups)
+        def _():
+            across_far(g + 1)
+
+        other = keys_values.at[g, :, rows_at(1 - my_y, half_tokens)]
+        whole(other, y_recv.at[g]).wait()
+        whole(queries.at[g], q_recv.at[g]).wait()
+        attention(g)
+        send_back(g)
+
+        @pl.when(g >= 1)
+        def _():
             pass_on(g - 1)
-        if g >= 2:
+
+        @pl.when(g >= 2)
+        def _():
             project_both(g - 2)
-    if groups >= 2:
-        project_both(groups - 2)
+
+        return carry
+
+    lax.fori_loop(0, groups, group, 0)
     last = groups - 1
+    project_both(last - 1)
     pass_on(last)
 
     load_res.wait()
@@ -293,8 +300,8 @@
     gate = mods[0, pl.ds(chosen, 1), :]
     mod_out[0:1, :] = mods[1, pl.ds(chosen, 1), :]
     mod_out[1:2, :] = mods[2, pl.ds(chosen, 1), :]
-    tile = rows // 3 if rows % 48 == 0 else 16
-    side = lax.broadcasted_iota(jnp.int32, (tile, 128), 1) < 64
+    strip = rows // 3 if rows % 48 == 0 else 16
+    side = lax.broadcasted_iota(jnp.int32, (strip, 128), 1) < 64
 
     def stats(half):
         part = rows_at(half, rows)
@@ -315,7 +322,7 @@
         project(last, half)
 
         def gated(i, carry):
-            at = rows_at(half * (rows // tile) + i, tile)
+            at = rows_at(half * (rows // strip) + i, strip)
             stream = res[at, :].astype(jnp.float32) + gate * acc[at, :]
             acc[at, :] = stream
             row_sum = jnp.sum(stream, axis=1, keepdims=True)
@@ -323,7 +330,7 @@
             stat_mine[at, :] = jnp.where(side, row_sum, row_sq)
             return carry
 
-        lax.fori_loop(0, rows // tile, gated, 0)
+        lax.fori_loop(0, rows // strip, gated, 0)
         stats(half).start()
         store(half).start()
 
@@ -333,12 +340,15 @@
     finish(1 - mp_i)
 
     whole(counts.at[pl.ds(0, 8 * (n - 1))], cnt_send).wait()
-    for g in range(groups):
-        for part in range(2):
-            sent = part_of(qkv, g, part).at[:, pl.ds(0, rows * (n - 1))]
-            whole(sent, qkv_send.at[g, part]).wait()
-        whole(obuf.at[g, pl.ds(0, rows * (n - 1))], o_send.at[g]).wait()
+
+    def drain(g, carry):
+        whole(obuf.at[g, pl.ds(0, rows * (row_n - 1))], o_send.at[g]).wait()
+        whole(keys_values.at[g, :, pl.ds(0, half_tokens)], y_send.at[g]).wait()
+        whole(queries.at[pl.ds(0, 3), pl.ds(0, rows * (row_n - 1))], x_send.at[g]).wait()
         whole(att.at[g, rows_at(mp_i, rows)], fwd_send.at[g]).wait()
+        return carry
+
+    lax.fori_loop(0, groups, drain, 0)
     for half in range(2):
         stats(half).wait_recv()
     stat_out[...] = stat_mine[...] + stat_other[...]
@@ -390,7 +400,8 @@
     rows, width = queries.shape
     high, columns = residual.shape
     tokens = rows * n
-    groups = width // HEAD_DIM // n
+    row_n = n // 2
+    groups = width // HEAD_DIM // row_n
     steps = modulation.shape[0]
     bf16, f32 = jnp.bfloat16, jnp.float32
     dma = pltpu.SemaphoreType.DMA
@@ -408,23 +419,23 @@
         out_specs=(hbm, vmem, vmem),
         scratch_shapes=[
             pltpu.VMEM((high, columns), f32),
-            pltpu.VMEM((groups, 3, n, rows, HEAD_DIM), bf16),
-            pltpu.VMEM((groups, 3, tokens, HEAD_DIM), bf16),
+            pltpu.VMEM((groups, 2, tokens, HEAD_DIM), bf16),
+            pltpu.VMEM((groups, tokens // 2, HEAD_DIM), bf16),
             pltpu.VMEM((tokens, HEAD_DIM), bf16),
             pltpu.VMEM((tokens, HEAD_DIM), bf16),
             pltpu.VMEM((HEAD_DIM + 16, tokens), bf16),
-            pltpu.VMEM((groups, tokens, HEAD_DIM), bf16),
-            pltpu.VMEM((groups, high, n * HEAD_DIM), bf16),
-            pltpu.VMEM((groups, n * HEAD_DIM, columns), bf16),
+            pltpu.VMEM((groups, tokens // 2, HEAD_DIM), bf16),
+            pltpu.VMEM((groups, high, row_n * HEAD_DIM), bf16),
+            pltpu.VMEM((groups, row_n * HEAD_DIM, columns), bf16),
             pltpu.VMEM((high, columns), bf16),
             pltpu.VMEM((3, steps, columns), f32),
             pltpu.VMEM((1, rows), jnp.int32),
             pltpu.VMEM((8 * n, 128), f32),
             pltpu.VMEM((high, 128), f32),
             pltpu.VMEM((high, 128), f32),
-            dma((groups, 2)), dma((groups, 2)), dma((groups,)), dma((groups,)),
-            dma((groups,)), dma((groups, n)), dma((groups,)), dma((groups,)),
-            dma, dma, dma((2,)), dma((2,)), dma((groups,)), dma((3,)),
+            dma((groups,)), dma((groups, row_n)), dma((groups,)), dma((groups,)),
+            dma((groups,)), dma((groups,)), dma((groups, row_n)), dma((groups,)),
+            dma((groups,)), dma, dma, dma((2,)), dma((2,)), dma((groups,)), dma((3,)),
             dma((2,)),
         ],
         compiler_params=pltpu.CompilerParams(
@@ -555,7 +566,8 @@
     def run(*arrays):
         queries = arrays[1]
         rows, width = queries.shape
-        if mp_n == 2 and width // HEAD_DIM % n == 0 and rows % 64 == 0 and rows * n % 512 == 0:
+        even = rows % 64 == 0 and rows * n % 512 == 0 and width // HEAD_DIM % (n // 2) == 0
+        if mp_n == 2 and seq_n == 4 and even and width // HEAD_DIM // (n // 2) >= 3:
             return fused(n, mp_n, *arrays)
         return local(*arrays)
 

time: 76.7 us -> 91.4 us (1.19)
  Pallas kernels: 74.6 us -> 89.9 us
    pallas_call x1, Pallas kernels: 71.4 us -> 86.7 us  [fused(): pl.pallas_call(functools.partial(fused_kernel, n, mp_n), out_shape=(jax.S...]
where the time goes in v4:
time: 91.4 us; the launch traced here: 91.2 us
  Pallas kernels  89.9 us (98%)
  between operations  1.29 us (1%)
    pallas_call x1, Pallas kernels, fused(): pl.pallas_call(functools.partial(fused_kernel, n, mp_n), out_shape=(jax.S...  86.7 us
    pallas_call x1, Pallas kernels, fused(): pl.pallas_call(functools.partial(norm_kernel, width), out_shape=(out, out...  3.2 us

profile of v4, /device:TPU:0, one launch (start us, length us, event | category | flops | bytes accessed | tf_op | source)
XLA Modules:
  0.0 91.2 jit_solution(3805363345670470000)
XLA Ops:
  1.3 86.7 %shard_map.95 = (f32[384,1536]{1,0:T(8,128)}, f32[384,128]{1,0:T(8,128)}, f32[2,1536]{1,0:T(2,128)}) custom-call(bf16[192,3072]{1,0:T(8,128)(2,1)} %q_ref.1, bf16[192,3072]{1,0:T(8,128)(2,1)} %k_ref.1, bf16[192,3072]{1,0:T(8,128)(2,1)} %v_ref.1, s32[1,192]{1,0:T(1,128)} %bitcast.3, s32[1]{0:T(128)S(6)} %copy.10.step_ref, f32[3,50,1536]{2,1,0:T(8,128)} %bitcast.2, ...), custom_call_target="tpu_custom_call" | custom-call | tf_op jit(solution)/shard_map/pallas_call | solution.py:411
  88.0 3.2 %shard_map.96 = (bf16[384,1536]{1,0:T(8,128)(2,1)}, bf16[384,1536]{1,0:T(8,128)(2,1)}) custom-call(f32[384,1536]{1,0:T(8,128)} %get-tuple-element.5.stream_ref, f32[384,128]{1,0:T(8,128)} %get-tuple-element.6.stat_ref, f32[2,1536]{1,0:T(2,128)} %get-tuple-element.7.mod_ref), custom_call_target="tpu_custom_call" | custom-call | tf_op jit(solution)/shard_map/pallas_call | solution.py:449

commit v5 on v3

--- a/solution.py
+++ b/solution.py
@@ -25,9 +25,9 @@
     n, mp_n,
     q_ref, k_ref, v_ref, ids_ref, step_ref, mod_ref, res_ref, w_ref,
     stream_ref, stat_out, mod_out,
-    acc, stage, qkv, key_marks, query_marks, values_t, obuf, att, wbuf, res, mods, ids_mine, counts,
+    acc, qkv, key_marks, query_marks, values_t, obuf, att, wbuf, res, mods, ids_mine, counts,
     stat_mine, stat_other,
-    stage_sem, qkv_send, kq_recv, v_recv, o_send, o_recv, fwd_send, fwd_recv,
+    qkv_send, qkv_recv, o_send, o_recv, fwd_send, fwd_recv,
     cnt_send, cnt_recv, stat_send, stat_recv, w_sem, in_sem, out_sem,
 ):
     seq_i = lax.axis_index("seq")
@@ -56,50 +56,25 @@
 
         lax.fori_loop(0, n, step, 0)
 
-    sources = (k_ref, q_ref, v_ref)
-    slots = ((0, 1), (2,))
-
-    def part_recv(g, part):
-        return (kq_recv, v_recv)[part].at[g]
-
-    def load_part(g, part):
-        for t in slots[part]:
-
-            def load(p, t=t):
-                pltpu.make_async_copy(
-                    sources[t].at[:, rows_at(p * groups + g, HEAD_DIM)],
-                    stage.at[g, t, p],
-                    stage_sem.at[g, part],
-                ).start()
-
-            every(load)
-            pltpu.make_async_copy(
-                sources[t].at[:, rows_at(me * groups + g, HEAD_DIM)],
-                qkv.at[g, t, rows_at(me, rows)],
-                part_recv(g, part),
-            ).start()
-
-    def part_of(ref, g, part):
-        return ref.at[g, pl.ds(slots[part][0], len(slots[part]))]
-
-    def send_part(g, part):
-        whole(part_of(stage, g, part), stage_sem.at[g, part]).wait()
-        for t in slots[part]:
-
-            def send(p, t=t):
+    def send_group(g):
+        for t, ref in enumerate((k_ref, q_ref, v_ref)):
+
+            def send(p, ref=ref, t=t):
                 pltpu.make_async_remote_copy(
-                    src_ref=stage.at[g, t, p],
+                    src_ref=ref.at[:, rows_at(p * groups + g, HEAD_DIM)],
                     dst_ref=qkv.at[g, t, rows_at(me, rows)],
-                    send_sem=qkv_send.at[g, part],
-                    recv_sem=part_recv(g, part),
+                    send_sem=qkv_send.at[g],
+                    recv_sem=qkv_recv.at[g],
                     device_id=device(p),
                     device_id_type=MESH,
                 ).start()
 
             each_peer(send)
-
-    def wait_part(g, part):
-        whole(part_of(qkv, g, part), part_recv(g, part)).wait()
+            pltpu.make_async_copy(
+                ref.at[:, rows_at(me * groups + g, HEAD_DIM)],
+                qkv.at[g, t, rows_at(me, rows)],
+                qkv_recv.at[g],
+            ).start()
 
     barrier = pltpu.get_barrier_semaphore()
     each_peer(
@@ -107,21 +82,15 @@
             barrier, inc=1, device_id=device(p), device_id_type=MESH
         )
     )
-    load_part(0, 0)
-    load_part(0, 1)
     load_ids = pltpu.make_async_copy(ids_ref, ids_mine, in_sem.at[0])
     load_res = pltpu.make_async_copy(res_ref, res, in_sem.at[1])
     load_mods = pltpu.make_async_copy(mod_ref, mods, in_sem.at[2])
     load_ids.start()
-    for g in range(1, groups):
-        load_part(g, 0)
-        load_part(g, 1)
     pl.semaphore_wait(barrier, n - 1)
 
-    order = [(g, part) for g in range(groups) for part in range(2)]
-    ahead = 3
-    for g, part in order[:ahead]:
-        send_part(g, part)
+    ahead = 2
+    for g in range(min(ahead, groups)):
+        send_group(g)
 
     load_ids.wait()
     ids = ids_mine[...]
@@ -272,11 +241,9 @@
         project(g, 1 - mp_i)
 
     for g in range(groups):
-        for part in range(2):
-            wait_part(g, part)
-            later = 2 * g + part + ahead
-            if later < len(order):
-                send_part(*order[later])
+        whole(qkv.at[g], qkv_recv.at[g]).wait()
+        if g + ahead < groups:
+            send_group(g + ahead)
         attend_and_send(g)
         if g >= 1:
             pass_on(g - 1)
@@ -334,9 +301,7 @@
 
     whole(counts.at[pl.ds(0, 8 * (n - 1))], cnt_send).wait()
     for g in range(groups):
-        for part in range(2):
-            sent = part_of(qkv, g, part).at[:, pl.ds(0, rows * (n - 1))]
-            whole(sent, qkv_send.at[g, part]).wait()
+        whole(qkv.at[g, :, pl.ds(0, rows * (n - 1))], qkv_send.at[g]).wait()
         whole(obuf.at[g, pl.ds(0, rows * (n - 1))], o_send.at[g]).wait()
         whole(att.at[g, rows_at(mp_i, rows)], fwd_send.at[g]).wait()
     for half in range(2):
@@ -408,7 +373,6 @@
         out_specs=(hbm, vmem, vmem),
         scratch_shapes=[
             pltpu.VMEM((high, columns), f32),
-            pltpu.VMEM((groups, 3, n, rows, HEAD_DIM), bf16),
             pltpu.VMEM((groups, 3, tokens, HEAD_DIM), bf16),
             pltpu.VMEM((tokens, HEAD_DIM), bf16),
             pltpu.VMEM((tokens, HEAD_DIM), bf16),
@@ -422,7 +386,7 @@
             pltpu.VMEM((8 * n, 128), f32),
             pltpu.VMEM((high, 128), f32),
             pltpu.VMEM((high, 128), f32),
-            dma((groups, 2)), dma((groups, 2)), dma((groups,)), dma((groups,)),
+            dma((groups,)), dma((groups,)),
             dma((groups,)), dma((groups, n)), dma((groups,)), dma((groups,)),
             dma, dma, dma((2,)), dma((2,)), dma((groups,)), dma((3,)),
             dma((2,)),

time: 76.7 us -> 77.1 us (level)
  no operation moved by 1% of the time
where the time goes in v5:
time: 77.1 us; the launch traced here: 76.2 us
  Pallas kernels  75 us (97%)
  between operations  1.29 us (2%)
    pallas_call x1, Pallas kernels, fused(): pl.pallas_call(functools.partial(fused_kernel, n, mp_n), out_shape=(jax.S...  71.8 us
    pallas_call x1, Pallas kernels, fused(): pl.pallas_call(functools.partial(norm_kernel, width), out_shape=(out, out...  3.2 us

profile of v5, /device:TPU:0, one launch (start us, length us, event | category | flops | bytes accessed | tf_op | source)
XLA Modules:
  0.0 76.2 jit_solution(6396139187651769509)
XLA Ops:
  1.3 71.8 %shard_map.95 = (f32[384,1536]{1,0:T(8,128)}, f32[384,128]{1,0:T(8,128)}, f32[2,1536]{1,0:T(2,128)}) custom-call(bf16[192,3072]{1,0:T(8,128)(2,1)} %q_ref.1, bf16[192,3072]{1,0:T(8,128)(2,1)} %k_ref.1, bf16[192,3072]{1,0:T(8,128)(2,1)} %v_ref.1, s32[1,192]{1,0:T(1,128)} %bitcast.3, s32[1]{0:T(128)S(6)} %copy.10.step_ref, f32[3,50,1536]{2,1,0:T(8,128)} %bitcast.2, ...), custom_call_target="tpu_custom_call" | custom-call | tf_op jit(solution)/shard_map/pallas_call | solution.py:365
  73.0 3.2 %shard_map.96 = (bf16[384,1536]{1,0:T(8,128)(2,1)}, bf16[384,1536]{1,0:T(8,128)(2,1)}) custom-call(f32[384,1536]{1,0:T(8,128)} %get-tuple-element.5.stream_ref, f32[384,128]{1,0:T(8,128)} %get-tuple-element.6.stat_ref, f32[2,1536]{1,0:T(2,128)} %get-tuple-element.7.mod_ref), custom_call_target="tpu_custom_call" | custom-call | tf_op jit(solution)/shard_map/pallas_call | solution.py:402

commit v6 on v5

--- a/solution.py
+++ b/solution.py
@@ -42,12 +42,24 @@
     def device(p):
         return {"seq": lax.div(p, mp_n), "mp": lax.rem(p, mp_n)}
 
+    x, y = lax.rem(seq_i, 2), lax.div(seq_i, 2)
+    beside = y * 2 + 1 - x
+    opposite = (1 - y) * 2 + x
+    across = (1 - y) * 2 + 1 - x
+    first = beside + mp_i * (opposite - beside)
+    second = opposite + mp_i * (beside - opposite)
+    peers_in_turn = [
+        chip * mp_n + core
+        for chip, core in (
+            (first, mp_i), (second, 1 - mp_i), (across, mp_i),
+            (first, 1 - mp_i), (second, mp_i), (across, 1 - mp_i),
+            (seq_i, 1 - mp_i),
+        )
+    ]
+
     def each_peer(body):
-        def step(d, carry):
-            body(lax.rem(me + d, n))
-            return carry
-
-        lax.fori_loop(1, n, step, 0)
+        for p in peers_in_turn:
+            body(p)
 
     def every(body):
         def step(p, carry):
@@ -519,7 +531,7 @@
     def run(*arrays):
         queries = arrays[1]
         rows, width = queries.shape
-        if mp_n == 2 and width // HEAD_DIM % n == 0 and rows % 64 == 0 and rows * n % 512 == 0:
+        if mp_n == 2 and seq_n == 4 and width // HEAD_DIM % n == 0 and rows % 64 == 0 and rows * n % 512 == 0:
             return fused(n, mp_n, *arrays)
         return local(*arrays)
 

time: 77.1 us -> 76.8 us (level)
  no operation moved by 1% of the time
where the time goes in v6:
time: 76.8 us; the launch traced here: 76 us
  Pallas kernels  74.8 us (97%)
  between operations  1.29 us (2%)
    pallas_call x1, Pallas kernels, fused(): pl.pallas_call(functools.partial(fused_kernel, n, mp_n), out_shape=(jax.S...  71.6 us
    pallas_call x1, Pallas kernels, fused(): pl.pallas_call(functools.partial(norm_kernel, width), out_shape=(out, out...  3.2 us

profile of v6, /device:TPU:0, one launch (start us, length us, event | category | flops | bytes accessed | tf_op | source)
XLA Modules:
  0.0 76.0 jit_solution(7264823198577672771)
XLA Ops:
  1.3 71.6 %shard_map.95 = (f32[384,1536]{1,0:T(8,128)}, f32[384,128]{1,0:T(8,128)}, f32[2,1536]{1,0:T(2,128)}) custom-call(bf16[192,3072]{1,0:T(8,128)(2,1)} %q_ref.1, bf16[192,3072]{1,0:T(8,128)(2,1)} %k_ref.1, bf16[192,3072]{1,0:T(8,128)(2,1)} %v_ref.1, s32[1,192]{1,0:T(1,128)} %bitcast.3, s32[1]{0:T(128)S(6)} %copy.10.step_ref, f32[3,50,1536]{2,1,0:T(8,128)} %bitcast.2, ...), custom_call_target="tpu_custom_call" | custom-call | tf_op jit(solution)/shard_map/pallas_call | solution.py:377
  72.8 3.2 %shard_map.96 = (bf16[384,1536]{1,0:T(8,128)(2,1)}, bf16[384,1536]{1,0:T(8,128)(2,1)}) custom-call(f32[384,1536]{1,0:T(8,128)} %get-tuple-element.5.stream_ref, f32[384,128]{1,0:T(8,128)} %get-tuple-element.6.stat_ref, f32[2,1536]{1,0:T(2,128)} %get-tuple-element.7.mod_ref), custom_call_target="tpu_custom_call" | custom-call | tf_op jit(solution)/shard_map/pallas_call | solution.py:414

commit v7 on v1

--- a/solution.py
+++ b/solution.py
@@ -112,31 +112,32 @@
         tile = 2 * HEAD_DIM
         factor = math.log2(math.e) / HEAD_DIM**0.5
 
-        def step(i, carry):
-            at = rows_at(i, tile)
-            place = (lax.broadcasted_iota(jnp.int32, (tile, 1), 0) + i * tile).astype(
+        reach = tokens // 2
+        for first in range(0, tokens, tile):
+            at = pl.ds(first, tile)
+            low = max(0, first - reach)
+            high = min(tokens, first + tile + reach)
+            near = pl.ds(low, high - low)
+            place = (lax.broadcasted_iota(jnp.int32, (tile, 1), 0) + first).astype(
                 jnp.float32
             )
             own_ids = sum((place >= c).astype(jnp.float32) for c in totals)
             score = lax.dot_general(
                 qkv[g, 1, at, :],
-                qkv[g, 0],
+                qkv[g, 0, near, :],
                 (((1,), (1,)), ((), ())),
                 preferred_element_type=jnp.float32,
             )
-            score = jnp.where(own_ids == key_ids, score, -1e30)
+            score = jnp.where(own_ids == key_ids[:, low:high], score, -1e30)
             top = jnp.max(score, axis=1, keepdims=True)
             weight = jnp.exp2((score - top) * factor)
             total = jnp.sum(weight, axis=1, keepdims=True)
             summed = jnp.dot(
                 weight.astype(jnp.bfloat16),
-                qkv[g, 2],
+                qkv[g, 2, near, :],
                 preferred_element_type=jnp.float32,
             )
             obuf[g, at, :] = (summed / total).astype(jnp.bfloat16)
-            return carry
-
-        lax.fori_loop(0, tokens // tile, step, 0)
 
     def send_back(g):
         def send(p):
@@ -183,7 +184,7 @@
             part = jnp.dot(
                 att[g], wbuf[g, :, at], preferred_element_type=jnp.float32
             )
-            acc[:, at] = part if g == 0 else acc[:, at] + part
+            acc[:, at] += part
             return carry
 
         lax.fori_loop(0, columns // tile, step, 0)
@@ -205,16 +206,29 @@
         sums = sums + counts[pl.ds(8 * r, 8), :]
     totals = [sums[k : k + 1, 0:1] for k in range(VIDEOS - 1)]
 
-    for g in range(groups):
+    acc[...] = jnp.zeros_like(acc)
+
+    def group(g, carry):
         whole(qkv.at[g], qkv_recv.at[g]).wait()
-        if g + 2 < groups:
+
+        @pl.when(g + 2 < groups)
+        def _():
             send_group(g + 2)
+
         attention(g, totals)
         send_back(g)
-        if g >= 1:
+
+        @pl.when(g >= 1)
+        def _():
             pass_on(g - 1)
-        if g >= 2:
+
+        @pl.when(g >= 2)
+        def _():
             project(g - 2)
+
+        return carry
+
+    lax.fori_loop(0, groups, group, 0)
     if groups >= 2:
         project(groups - 2)
     pass_on(groups - 1)

time: 74.4 us -> 72.7 us (0.977)
  Pallas kernels: 68.6 us -> 66.9 us
    pallas_call x1, Pallas kernels: 68.6 us -> 66.9 us  [fused(): pl.pallas_call(functools.partial(fused_kernel, n, mp_n, width), out_shape...]
where the time goes in v7:
time: 72.7 us; the launch traced here: 72.2 us
  Pallas kernels  66.9 us (92%)
  local copies, waits for them, and re-layouts  3.9 us (5%)
  between operations  1.41 us (2%)
    pallas_call x1, Pallas kernels, fused(): pl.pallas_call(functools.partial(fused_kernel, n, mp_n, width), out_shape...  66.9 us
    unnamed x9, local copies, waits for them, and re-layouts  3.88 us

profile of v7, /device:TPU:0, one launch (start us, length us, event | category | flops | bytes accessed | tf_op | source)
XLA Modules:
  0.0 72.2 jit_solution(5980518511772737774)
XLA Ops:
  0.6 0.0 copy-start
  1.4 0.5 copy-done
  1.9 0.0 copy-start.1
  1.9 0.7 copy-done.1
  2.6 66.9 %shard_map.95 = (bf16[384,1536]{1,0:T(8,128)(2,1)S(1)}, bf16[384,1536]{1,0:T(8,128)(2,1)}) custom-call(bf16[192,3072]{1,0:T(8,128)(2,1)} %q_ref.1, bf16[192,3072]{1,0:T(8,128)(2,1)} %k_ref.1, bf16[192,3072]{1,0:T(8,128)(2,1)} %v_ref.1, s32[1,192]{1,0:T(1,128)S(1)} %bitcast.9, f32[3,1536]{1,0:T(4,128)S(1)} %bitcast.8, bf16[384,1536]{1,0:T(8,128)(2,1)} %res_ref.1, ...), custom_call_target="tpu_custom_call" | custom-call | tf_op jit(solution)/shard_map/pallas_call | solution.py:304
  69.5 0.0 copy-start.2
  69.5 1.0 %copy.16 = bf16[384,1536]{1,0:T(8,128)(2,1)} copy(bf16[384,1536]{1,0:T(8,128)(2,1)S(1)} %get-tuple-element.4) | data formatting | bytes 2359296
  70.5 0.7 copy-done.2
  71.2 1.0 %copy.17 = bf16[384,1536]{1,0:T(8,128)(2,1)} copy(bf16[384,1536]{1,0:T(8,128)(2,1)S(1)} %copy-done.2) | data formatting | bytes 2359296
  (2 shorter events, 0.0 us)
Async XLA Ops:
  0.6 1.2 %copy-start = (f32[50,3,1536]{2,0,1:T(8,128)S(1)}, f32[50,3,1536]{2,0,1:T(8,128)}, u32[]{:S(2)}) copy-start(f32[50,3,1536]{2,0,1:T(8,128)} %param.14) | copy-start | bytes 2764804
  1.9 0.7 copy-start.1
  69.5 1.7 %copy-start.2 = (bf16[384,1536]{1,0:T(8,128)(2,1)S(1)}, bf16[384,1536]{1,0:T(8,128)(2,1)}, u32[]{:S(2)}) copy-start(bf16[384,1536]{1,0:T(8,128)(2,1)} %get-tuple-element.5) | copy-start | bytes 3538948

commit v8 on v7

--- a/solution.py
+++ b/solution.py
@@ -106,14 +106,14 @@
                 qkv_recv.at[g],
             ).start()
 
-    def attention(g, totals):
+    def attention(g, totals, part):
         lane = lax.broadcasted_iota(jnp.int32, (1, tokens), 1).astype(jnp.float32)
         key_ids = sum((lane >= c).astype(jnp.float32) for c in totals)
         tile = 2 * HEAD_DIM
         factor = math.log2(math.e) / HEAD_DIM**0.5
 
         reach = tokens // 2
-        for first in range(0, tokens, tile):
+        for first in range(part * reach, (part + 1) * reach, tile):
             at = pl.ds(first, tile)
             low = max(0, first - reach)
             high = min(tokens, first + tile + reach)
@@ -139,25 +139,32 @@
             )
             obuf[g, at, :] = (summed / total).astype(jnp.bfloat16)
 
-    def send_back(g):
-        def send(p):
-            pltpu.make_async_remote_copy(
-                src_ref=obuf.at[g, rows_at(p, rows)],
-                dst_ref=att.at[
-                    g, rows_at(lax.rem(p, mp_n), rows), rows_at(me, HEAD_DIM)
-                ],
-                send_sem=o_send.at[g],
-                recv_sem=o_recv.at[g],
-                device_id=device(p),
-                device_id_type=MESH,
-            ).start()
-
-        each_peer(send)
-        pltpu.make_async_copy(
-            obuf.at[g, rows_at(me, rows)],
-            att.at[g, rows_at(mp_i, rows), rows_at(me, HEAD_DIM)],
-            o_recv.at[g],
-        ).start()
+    def send_back(g, part):
+        half = n // 2
+
+        def send(d, carry):
+            p = part * half + lax.rem(me + d, half)
+            block = obuf.at[g, rows_at(p, rows)]
+            there = att.at[g, rows_at(lax.rem(p, mp_n), rows), rows_at(me, HEAD_DIM)]
+
+            @pl.when(p != me)
+            def _():
+                pltpu.make_async_remote_copy(
+                    src_ref=block,
+                    dst_ref=there,
+                    send_sem=o_send.at[g],
+                    recv_sem=o_recv.at[g],
+                    device_id=device(p),
+                    device_id_type=MESH,
+                ).start()
+
+            @pl.when(p == me)
+            def _():
+                pltpu.make_async_copy(block, there, o_recv.at[g]).start()
+
+            return carry
+
+        lax.fori_loop(0, half, send, 0)
 
     def forward(g):
         half = att.at[g, rows_at(mp_i, rows)]
@@ -215,8 +222,9 @@
         def _():
             send_group(g + 2)
 
-        attention(g, totals)
-        send_back(g)
+        for part in range(2):
+            attention(g, totals, part)
+            send_back(g, part)
 
         @pl.when(g >= 1)
         def _():
@@ -430,7 +438,7 @@
     def run(*arrays):
         queries = arrays[1]
         rows, width = queries.shape
-        if mp_n == 2 and width // HEAD_DIM % n == 0 and rows % 64 == 0 and rows * n % 256 == 0:
+        if mp_n == 2 and width // HEAD_DIM % n == 0 and rows % 64 == 0 and rows * n % 512 == 0:
             return fused(n, mp_n, *arrays)
         return local(*arrays)
 

time: 72.7 us -> 71.3 us (0.981)
  Pallas kernels: 66.9 us -> 65.8 us
    pallas_call x1, Pallas kernels: 66.9 us -> 65.8 us  [fused(): pl.pallas_call(functools.partial(fused_kernel, n, mp_n, width), out_shape...]
where the time goes in v8:
time: 71.3 us; the launch traced here: 71.1 us
  Pallas kernels  65.8 us (92%)
  local copies, waits for them, and re-layouts  3.9 us (5%)
  between operations  1.41 us (2%)
    pallas_call x1, Pallas kernels, fused(): pl.pallas_call(functools.partial(fused_kernel, n, mp_n, width), out_shape...  65.8 us
    unnamed x9, local copies, waits for them, and re-layouts  3.88 us

profile of v8, /device:TPU:0, one launch (start us, length us, event | category | flops | bytes accessed | tf_op | source)
XLA Modules:
  0.0 71.1 jit_solution(9371145666558957211)
XLA Ops:
  0.6 0.0 copy-start
  1.4 0.5 copy-done
  1.9 0.0 copy-start.1
  1.9 0.7 copy-done.1
  2.6 65.8 %shard_map.95 = (bf16[384,1536]{1,0:T(8,128)(2,1)S(1)}, bf16[384,1536]{1,0:T(8,128)(2,1)}) custom-call(bf16[192,3072]{1,0:T(8,128)(2,1)} %q_ref.1, bf16[192,3072]{1,0:T(8,128)(2,1)} %k_ref.1, bf16[192,3072]{1,0:T(8,128)(2,1)} %v_ref.1, s32[1,192]{1,0:T(1,128)S(1)} %bitcast.9, f32[3,1536]{1,0:T(4,128)S(1)} %bitcast.8, bf16[384,1536]{1,0:T(8,128)(2,1)} %res_ref.1, ...), custom_call_target="tpu_custom_call" | custom-call | tf_op jit(solution)/shard_map/pallas_call | solution.py:312
  68.4 0.0 copy-start.2
  68.4 1.0 %copy.16 = bf16[384,1536]{1,0:T(8,128)(2,1)} copy(bf16[384,1536]{1,0:T(8,128)(2,1)S(1)} %get-tuple-element.4) | data formatting | bytes 2359296
  69.5 0.7 copy-done.2
  70.1 1.0 %copy.17 = bf16[384,1536]{1,0:T(8,128)(2,1)} copy(bf16[384,1536]{1,0:T(8,128)(2,1)S(1)} %copy-done.2) | data formatting | bytes 2359296
  (2 shorter events, 0.0 us)
Async XLA Ops:
  0.6 1.2 %copy-start = (f32[50,3,1536]{2,0,1:T(8,128)S(1)}, f32[50,3,1536]{2,0,1:T(8,128)}, u32[]{:S(2)}) copy-start(f32[50,3,1536]{2,0,1:T(8,128)} %param.14) | copy-start | bytes 2764804
  1.9 0.7 copy-start.1
  68.4 1.7 %copy-start.2 = (bf16[384,1536]{1,0:T(8,128)(2,1)S(1)}, bf16[384,1536]{1,0:T(8,128)(2,1)}, u32[]{:S(2)}) copy-start(bf16[384,1536]{1,0:T(8,128)(2,1)} %get-tuple-element.5) | copy-start | bytes 3538948
